TPU v7x, 128 devices: a whole 4x4x4 slice. The times are simulated.
128 devices in a mesh: grp: 16 (over y, x), head: 8 (over z, core).
Axes of the slice: x: 4, y: 4, z: 4, core: 2. Of those that a mesh axis runs over, the one named last changes fastest.
Arguments:
- resident_cache: bfloat16 [16, 8, 1536, 576], P('grp'), may hold values from -4 to 4
- lengths: int32 [16, 8], P('grp'), may hold values from 1 to 1536, 7680 in all within a row
- slices: bfloat16 [256, 64, 576], P('grp'), may hold values from -4 to 4
- placement: int32 [256, 1], P('grp'), may hold values from 0 to 15; in each aligned block of 16 rows (0 to 15, 16 to 31, ...) at most 2 rows name the same one
- queries: bfloat16 [3, 16, 9, 24576], P(None, 'grp', None, 'head')
- latents: bfloat16 [3, 16, 9, 576], P(None, 'grp'), may hold values from -4 to 4
- w_key: bfloat16 [128, 128, 512], P('head'), may hold values from -0.5 to 0.5
- w_value: bfloat16 [128, 512, 128], P('head'), may hold values from -4 to 4
- w_out: bfloat16 [16384, 7168], P('head', 'grp'), may hold values from -0.046875 to 0.046875
Outputs:
- mixed: bfloat16 [3, 16, 9, 7168], P(None, 'grp', None, 'head')
Inputs may be any that keep to these rules, and one draw needn't show every extreme that they name: `placement`: among the 16 slices of one owner no decode group is named more than 2 times, a bound that some block reaches. `lengths`: the largest length in each group equals 1536.
All inputs are finite; a program needn't handle non-finite values.
Results may differ from a plain program's by a relative error of at most 0.019.
Values may be sent and summed in bfloat16 or wider, within the bound.
A program may use at most 192 MiB of HBM per device.

v0:
```python
import math

import jax
import jax.numpy as jnp
from jax import lax
from jax.sharding import PartitionSpec as P

KV = 512
ROPE = 64
NOPE = 128
VD = 128
ROWS = 8
LRES = 1536
SL = 64
CAP = 2
STEPS = 3


def prepare(question, w_key):
    absorbed = jnp.einsum(
        "trhd,hdc->trhc", question[..., :NOPE], w_key, preferred_element_type=jnp.float32
    ).astype(jnp.bfloat16)
    return jnp.concatenate([absorbed, question[..., NOPE:]], axis=-1)


def attend(asked, stored, stored_mask, recent, recent_mask):
    score_scale = 1.0 / math.sqrt(NOPE + ROPE)
    s_stored = (
        jnp.einsum("rhc,rlc->rhl", asked, stored, preferred_element_type=jnp.float32) * score_scale
    )
    s_stored = jnp.where(stored_mask[:, None, :], s_stored, -jnp.inf)
    s_recent = (
        jnp.einsum("rhc,rtc->rht", asked, recent, preferred_element_type=jnp.float32) * score_scale
    )
    s_recent = jnp.where(recent_mask[None, :, :], s_recent, -jnp.inf)
    highest = jnp.maximum(jnp.max(s_stored, axis=-1), jnp.max(s_recent, axis=-1))
    e_stored = jnp.exp(s_stored - highest[..., None])
    e_recent = jnp.exp(s_recent - highest[..., None])
    denominator = jnp.sum(e_stored, axis=-1) + jnp.sum(e_recent, axis=-1)
    p_stored = (e_stored / denominator[..., None]).astype(jnp.bfloat16)
    p_recent = (e_recent / denominator[..., None]).astype(jnp.bfloat16)
    latent = jnp.einsum(
        "rhl,rlc->rhc", p_stored, stored[..., :KV], preferred_element_type=jnp.float32
    )
    return latent + jnp.einsum(
        "rht,rtc->rhc", p_recent, recent[..., :KV], preferred_element_type=jnp.float32
    )


def pack_slices(portion, placement, groups):
    count = portion.shape[0]
    owners = placement[:, 0]
    alike = owners[:, None] == owners[None, :]
    before = jnp.arange(count)[:, None] < jnp.arange(count)[None, :]
    ranking = jnp.sum(alike & before, axis=0)
    target = owners * CAP + ranking
    selector = (jnp.arange(groups * CAP, dtype=jnp.int32)[:, None] == target[None, :]).astype(
        jnp.bfloat16
    )
    packed = jnp.dot(
        selector, portion.reshape(count, -1), preferred_element_type=jnp.float32
    ).astype(jnp.bfloat16)
    packed = packed.reshape(groups, CAP, portion.shape[1], portion.shape[2])
    filled = jnp.sum(selector.astype(jnp.float32), axis=1).astype(jnp.bfloat16).reshape(groups, CAP)
    return (packed, filled)


def body(resident_cache, lengths, slices, placement, queries, latents, w_key, w_value, w_out):
    groups = lax.axis_size("grp")
    heads_here = w_key.shape[0]
    packed, filled = pack_slices(slices, placement, groups)
    received, present = (
        lax.all_to_all(packed, "grp", split_axis=0, concat_axis=0, tiled=True),
        lax.all_to_all(filled, "grp", split_axis=0, concat_axis=0, tiled=True),
    )
    arrived = received.reshape(1, groups * CAP * SL, KV + ROPE)
    join_mask = jnp.broadcast_to((present > 0.5)[:, :, None], (groups, CAP, SL)).reshape(1, -1)
    stored = resident_cache[0]
    stored_mask = jnp.arange(LRES, dtype=jnp.int32)[None, :] < lengths[0][:, None]
    recent_all = jnp.swapaxes(latents[:, 0], 0, 1)
    question = queries[:, 0].reshape(STEPS, ROWS + 1, heads_here, NOPE + ROPE)
    prepared = prepare(question, w_key)
    prepared = jnp.transpose(prepared, (1, 0, 2, 3)).reshape(
        ROWS + 1, STEPS * heads_here, KV + ROPE
    )
    step_of = jnp.arange(STEPS * heads_here, dtype=jnp.int32) // heads_here
    recent_mask = jnp.arange(STEPS, dtype=jnp.int32)[None, :] <= step_of[:, None]
    upper = attend(prepared[:ROWS], stored, stored_mask, recent_all[:ROWS], recent_mask)
    lower = attend(prepared[ROWS:], arrived, join_mask, recent_all[ROWS:], recent_mask)
    latent = jnp.concatenate([upper, lower], axis=0).astype(jnp.bfloat16)
    latent = jnp.transpose(latent.reshape(ROWS + 1, STEPS, heads_here, KV), (1, 0, 2, 3))
    heads_out = jnp.einsum(
        "trhc,hcv->trhv", latent, w_value, preferred_element_type=jnp.float32
    ).astype(jnp.bfloat16)
    attended = heads_out.reshape(STEPS * (ROWS + 1), heads_here * VD)
    partial_sums = jnp.dot(
        attended,
        lax.all_gather(w_out, "grp", axis=1, tiled=True),
        preferred_element_type=jnp.float32,
    )
    summed = lax.psum_scatter(
        partial_sums.astype(jnp.bfloat16), "head", scatter_dimension=1, tiled=True
    )
    return summed.reshape(STEPS, 1, ROWS + 1, -1)


def solution(mesh):
    placed = (
        P("grp", None, None, None),
        P("grp", None),
        P("grp", None, None),
        P("grp", None),
        P(None, "grp", None, "head"),
        P(None, "grp", None, None),
        P("head", None, None),
        P("head", None, None),
        P("head", "grp"),
    )
    return jax.shard_map(
        body, mesh=mesh, in_specs=placed, out_specs=P(None, "grp", None, "head"), check_vma=False
    )
```

profile of v0, /device:TPU:1, one launch (start us, length us, event | category | flops | bytes accessed | tf_op | source)
XLA Modules:
  0.0 269.9 jit_solution(1631335587531388407)
XLA Ops:
  6.5 0.7 all-gather.2.cloned.1.call-update
  7.3 0.8 convert_reduce_fusion
  8.1 0.7 multiply_add_fusion
  8.8 0.7 all_to_all.12
  9.5 7.6 %all-to-all-start = ((bf16[16,1,2]{2,1,0:T(2,128)(2,1)}), bf16[16,1,2]{2,1,0:T(2,128)(2,1)S(1)}, u32[]{:S(2)}, u32[]{:S(2)}) async-start(bf16[16,1,2]{2,1,0:T(2,128)(2,1)} %all_to_all.12), calls=%async_computation | async-start | bytes 16384 | tf_op jit(solution)/shard_map/all_to_all | solution.py:74
  17.1 1.2 reshape_squeeze.3
  18.4 0.4 fusion.20
  18.8 0.2 maximum_bitcast_fusion
  19.1 2.7 reshape.182
  21.8 2.3 convolution_convert_fusion
  24.2 9.7 %fusion.56 = (f32[8,48]{1,0:T(8,128)S(1)}, f32[8,48,1536]{2,1,0:T(8,128)}) fusion(bf16[8,48,576]{2,1,0:T(8,128)(2,1)S(1)} %bitcast.80, bf16[1,8,1536,576]{2,3,1,0:T(8,128)(2,1)} %param.9, pred[8,1536]{1,0:T(8,128)(4,1)S(1)} %iota_compare_fusion), kind=kOutput, calls=%fused_computation.75 | convolution fusion | flops 681246336 | bytes 16971264 | tf_op jit(solution)/shard_map/rhc,rlc->rhl/dot_general | solution.py:29
  33.9 5.7 %reshape.183 = bf16[16,2,64,576]{3,2,1,0:T(8,128)(2,1)} reshape(bf16[32,36864]{1,0:T(8,128)(2,1)} %convolution_convert_fusion) | data formatting | bytes 4718592 | tf_op jit(solution)/shard_map/reshape | solution.py:63
  39.6 6.9 %all-to-all-start.1 = ((bf16[16,2,64,576]{3,2,1,0:T(8,128)(2,1)}), bf16[16,2,64,576]{3,2,1,0:T(8,128)(2,1)}, u32[]{:S(2)}, u32[]{:S(2)}) async-start(bf16[16,2,64,576]{3,2,1,0:T(8,128)(2,1)} %reshape.183), calls=%async_computation.1 | async-start | bytes 5242880 | tf_op jit(solution)/shard_map/all_to_all | solution.py:73
  46.4 0.2 reduce-scatter.4.cloned.1.call-start
  46.7 0.3 fusion.57
  46.9 18.8 %copy.58 = bf16[1,8,1536,576]{3,2,1,0:T(8,128)(2,1)} copy(bf16[1,8,1536,576]{2,3,1,0:T(8,128)(2,1)} %param.9) | data formatting | bytes 28311552 | tf_op args[0]
  65.8 2.3 fusion.16
  68.1 5.9 %fusion.2 = f32[8,48,512]{2,1,0:T(8,128)S(1)} fusion(bf16[8,1536,576]{2,1,0:T(8,128)(2,1)} %bitcast.78, f32[8,48,1536]{2,1,0:T(8,128)S(1)} %copy-done.2, f32[8,48]{1,0:T(8,128)S(1)} %add.37, f32[8,48]{1,0:T(8,128)S(1)} %max.16), kind=kOutput, calls=%fused_computation.3 | convolution fusion | flops 605749248 | bytes 15731712 | tf_op jit(solution)/shard_map/rhl,rlc->rhc/dot_general | solution.py:42
  74.0 0.3 fusion.23
  74.4 0.2 copy.64
  75.2 19.3 %all-to-all-done.1 = bf16[16,2,64,576]{3,2,1,0:T(8,128)(2,1)} async-done(((bf16[16,2,64,576]{3,2,1,0:T(8,128)(2,1)}), bf16[16,2,64,576]{3,2,1,0:T(8,128)(2,1)}, u32[]{:S(2)}, u32[]{:S(2)}) %all-to-all-start.1) | async-done | bytes 2359328 | tf_op jit(solution)/shard_map/all_to_all | solution.py:73
  94.4 3.5 %fusion.54 = (f32[48]{0:T(128)S(1)}, f32[48,2048]{1,0:T(8,128)S(1)}) fusion(bf16[48,576]{1,0:T(8,128)(2,1)S(1)} %bitcast.87, bf16[2048,576]{1,0:T(8,128)(2,1)} %bitcast.15, pred[2048]{0:T(1024)(128)(4,1)S(1)} %broadcast_in_dim.71), kind=kOutput, calls=%fused_computation.73 | convolution fusion | flops 113541072 | bytes 2810048 | tf_op jit(solution)/shard_map/rhc,rlc->rhl/dot_general | solution.py:29
  98.0 0.2 fusion.37
  98.2 2.3 fusion.11
  100.5 0.2 fusion.32
  100.8 0.5 fusion.29
  101.4 113.7 %all-gather.2.cloned.1.call-done = bf16[2048,7168]{0,1:T(8,128)(2,1)} async-done(((bf16[2048,448]{0,1:T(8,128)(2,1)}), bf16[2048,7168]{0,1:T(8,128)(2,1)}) %all-gather.2.cloned.1.call-update) | async-done | bytes 29360144 | tf_op jit(solution)/shard_map/all_gather | solution.py:98
  215.1 14.2 %convolution_convert_fusion.1 = bf16[27,7168]{1,0:T(8,128)(2,1)S(1)} fusion(bf16[27,2048]{1,0:T(8,128)(2,1)S(1)} %bitcast.83, bf16[2048,7168]{0,1:T(8,128)(2,1)} %all-gather.2.cloned.1.call-done), kind=kOutput, calls=%fused_computation.5 | convolution fusion | flops 792916992 | bytes 29857792 | tf_op jit(solution)/shard_map/dot_general | solution.py:96
  229.3 1.8 copy.73
  231.1 30.2 %reduce-scatter.4.cloned.1.call-done = bf16[896,27]{1,0:T(8,128)(2,1)} async-done(((bf16[7168,27]{1,0:T(8,128)(2,1)}), bf16[896,27]{1,0:T(8,128)(2,1)}) %reduce-scatter.4.cloned.1.call-update) | async-done | bytes 48400
  261.3 1.1 copy.74
  262.4 0.7 copy.67
  (43 shorter events, 1.3 us)
Async XLA Ops:
  6.5 11.9 %copy-start = (bf16[16,128,512]{2,1,0:T(8,128)(2,1)S(1)}, bf16[16,128,512]{2,1,0:T(8,128)(2,1)}, u32[]{:S(2)}) copy-start(bf16[16,128,512]{2,1,0:T(8,128)(2,1)} %param.15) | copy-start | bytes 6291460
  6.5 208.5 %all-gather.2.cloned.1.call-start = ((), (), s32[]{:S(2)}) async-start(), calls=%async_computation.3 | async-start | bytes 31195136 | tf_op jit(solution)/shard_map/all_gather | solution.py:98
  9.5 30.0 %all-to-all-start = ((bf16[16,1,2]{2,1,0:T(2,128)(2,1)}), bf16[16,1,2]{2,1,0:T(2,128)(2,1)S(1)}, u32[]{:S(2)}, u32[]{:S(2)}) async-start(bf16[16,1,2]{2,1,0:T(2,128)(2,1)} %all_to_all.12), calls=%async_computation | async-start | bytes 16384 | tf_op jit(solution)/shard_map/all_to_all | solution.py:74
  21.8 2.3 copy-start.4
  39.5 7.1 %copy-start.3 = (bf16[3,1,9,576]{3,0,2,1:T(4,128)(2,1)S(1)}, bf16[3,1,9,576]{3,0,2,1:T(4,128)(2,1)}, u32[]{:S(2)}) copy-start(bf16[3,1,9,576]{3,0,2,1:T(4,128)(2,1)} %param.14) | copy-start | bytes 93316
  39.6 54.9 %all-to-all-start.1 = ((bf16[16,2,64,576]{3,2,1,0:T(8,128)(2,1)}), bf16[16,2,64,576]{3,2,1,0:T(8,128)(2,1)}, u32[]{:S(2)}, u32[]{:S(2)}) async-start(bf16[16,2,64,576]{3,2,1,0:T(8,128)(2,1)} %reshape.183), calls=%async_computation.1 | async-start | bytes 5242880 | tf_op jit(solution)/shard_map/all_to_all | solution.py:73
  46.4 214.8 %reduce-scatter.4.cloned.1.call-start = ((), (), s32[]{:S(2)}) async-start(), calls=%async_computation.4 | async-start | bytes 2064384
  65.7 2.4 copy-start.2
  97.9 2.9 %copy-start.5 = (bf16[16,512,128]{2,1,0:T(8,128)(2,1)S(1)}, bf16[16,512,128]{2,1,0:T(8,128)(2,1)}, u32[]{:S(2)}) copy-start(bf16[16,512,128]{2,1,0:T(8,128)(2,1)} %param.16) | copy-start | bytes 6291460
  215.1 47.9 %copy-start.1 = (bf16[16,128,512]{2,1,0:T(8,128)(2,1)S(1)}, bf16[16,128,512]{2,1,0:T(8,128)(2,1)}, u32[]{:S(2)}) copy-start(bf16[16,128,512]{2,1,0:T(8,128)(2,1)} %param.15) | copy-start | bytes 6291460
Sparse Core Ops, SparseCore 0:
  9.5 205.5 all-gather.1
  231.2 30.0 reduce-scatter.3
where the time goes:
time: 273 us; the launch traced here: 270 us
  waiting for transfers between devices  164 us (60%)
  matrix products  39.6 us (15%)
  local copies, waits for them, and re-layouts  33.6 us (12%)
  starting transfers between devices  14.7 us (5%)
  between operations  13.7 us (5%)
  other arithmetic  4.4 us (2%)
    all_gather x1, waiting for transfers between devices, body(): lax.all_gather(w_out, 'grp', axis=1, tiled=True)  114 us
    unnamed x3, waiting for transfers between devices  30.9 us
    unnamed x18, local copies, waits for them, and re-layouts  21.8 us
    all_to_all x1, waiting for transfers between devices, body(): lax.all_to_all(packed, 'grp', split_axis=0, concat_axis=0, tiled=True)  19.3 us
    dot_general x1, matrix products, body(): jnp.dot(attended, lax.all_gather(w_out, 'grp', axis=1, tiled=True), prefe...  14.2 us
    dot_general x2, matrix products, attend(): jnp.einsum('rhc,rlc->rhl', asked, stored, preferred_element_type=jnp.floa...  13.2 us
    dot_general x2, matrix products, attend(): jnp.einsum('rhl,rlc->rhc', p_stored, stored[..., :KV], preferred_element_...  8.16 us
    all_to_all x1, starting transfers between devices, body(): lax.all_to_all(filled, 'grp', split_axis=0, concat_axis=0, tiled=True)  7.58 us
  transfers between devices with their start and end apart: 4, of which 3 were waited for; matrix products, arithmetic and copies ran while one was open for 22% of the time, Pallas kernels for 0%

commit v1 on v0

v1 whole, which is shorter than its diff:
```python
import functools
import math

import jax
import jax.numpy as jnp
from jax import lax
from jax.experimental import pallas as pl
from jax.experimental.pallas import tpu as pltpu
from jax.sharding import PartitionSpec as P

KV = 512
ROPE = 64
NOPE = 128
VD = 128
ROWS = 8
LRES = 1536
SL = 64
CAP = 2
STEPS = 3

MESH = pl.DeviceIdType.MESH
SCALE = 1.0 / math.sqrt(NOPE + ROPE)
LOWEST = float(jnp.finfo(jnp.float32).min)
BF16 = jnp.bfloat16
F32 = jnp.float32
WIDE = 640
PAD = 4
HEADS = 16
ASK = HEADS * PAD
TOK = 16


def remote(src, dst, send_sem, recv_sem, dev):
    return pltpu.make_async_remote_copy(
        src_ref=src, dst_ref=dst, send_sem=send_sem, recv_sem=recv_sem, device_id=dev, device_id_type=MESH
    )


def nt(a, b):
    return lax.dot_general(a, b, (((1,), (1,)), ((), ())), preferred_element_type=F32)


def nn(a, b):
    return jnp.dot(a, b, preferred_element_type=F32)


def step_mask(rows, width):
    step = lax.broadcasted_iota(jnp.int32, (rows, width), 0) % PAD
    at = lax.broadcasted_iota(jnp.int32, (rows, width), 1)
    return (at < STEPS) & (at <= step)


def kernel(
    lengths, code, queries, latents, cache, slices, w_key, w_value, w_out,
    out,
    kt, wk, wv, wo, sl, slw, k_send, qf, lat,
    q_all, q_sib, q8, k8, o_sib, lt, o8_send, o8, st_send, st8,
    gath, p_send, p_recv, p_sum, red,
    dma, sib_s, sib_r, sl_s, sl_r, z_s, z_r, ag_s, ag_r, red_s, red_r,
):
    g = lax.axis_index("grp")
    h = lax.axis_index("head")
    y, x = g // 4, g % 4
    z, c = h // 2, h % 2
    sib = (g, h + 1 - 2 * c)

    load_wk = pltpu.make_async_copy(w_key, wk, dma.at[0])
    load_sl = pltpu.make_async_copy(slices.at[:, pl.ds(TOK * z, TOK), :], sl, dma.at[1])
    load_kt = [pltpu.make_async_copy(cache.at[4 * c + i], kt.at[i], dma.at[2 + i]) for i in range(4)]
    load_wv = pltpu.make_async_copy(w_value, wv, dma.at[6])
    load_wo = pltpu.make_async_copy(w_out, wo, dma.at[7])
    load_sl.start()
    load_wk.start()
    for cp in load_kt:
        cp.start()
    load_wv.start()
    load_wo.start()

    barrier = pltpu.get_barrier_semaphore()
    for i in range(1, 16):
        pl.semaphore_signal(barrier, inc=1, device_id=((g + i) % 16, h), device_id_type=MESH)
    for i in range(1, 8):
        pl.semaphore_signal(barrier, inc=1, device_id=(g, (h + i) % 8), device_id_type=MESH)

    qf[...] = jnp.zeros_like(qf)
    lat[...] = jnp.zeros_like(lat)
    for r in range(ROWS + 1):
        v = queries[r].astype(F32)
        qf[r, 0:STEPS, :] = v
        qf[r, PAD : PAD + STEPS, :] = v
        lat[r, 0:STEPS, :] = latents[r].astype(F32)

    load_sl.wait()
    slw[:, KV:WIDE] = jnp.ones((16 * TOK, WIDE - KV), BF16)
    slw[:, 0 : KV + ROPE] = sl[...].reshape(16 * TOK, KV + ROPE)
    at0 = lax.broadcasted_iota(jnp.int32, (16 * TOK, 16 * TOK), 0)
    at1 = lax.broadcasted_iota(jnp.int32, (16 * TOK, 16 * TOK), 1)
    chosen = (at0 % TOK == at1 % TOK) & ((at0 // TOK) * CAP + c == code[0:1, :])
    selector = jnp.where(chosen, 1.0, 0.0).astype(BF16)
    k_send[...] = nn(selector, slw[...]).astype(BF16).reshape(16, TOK, WIDE)

    pl.semaphore_wait(barrier, 22)

    slice_sends = []
    for i in range(1, 16):
        to = (g + i) % 16
        cp = remote(k_send.at[to], k8.at[c, pl.ds(TOK * g, TOK)], sl_s.at[i], sl_r.at[i], (to, h))
        cp.start()
        slice_sends.append(cp)
    k8[c, pl.ds(TOK * g, TOK), :] = k_send[g]

    load_wk.wait()
    row = lax.broadcasted_iota(jnp.int32, (72, 128), 0)
    lane = lax.broadcasted_iota(jnp.int32, (72, 128), 1)
    first = row % 8 < PAD
    low = lane < ROPE
    for quad in range(4):
        parts = []
        for p in (2 * quad, 2 * quad + 1):
            t = qf[:, :, 384 * p : 384 * p + 384].reshape(72, 384)
            t0, t1, t2 = t[:, 0:128], t[:, 128:256], t[:, 256:384]
            r1, r2 = pltpu.roll(t1, 64, 1), pltpu.roll(t2, 64, 1)
            second_nope = jnp.where(low, r1, r2)
            rope = jnp.where(low, jnp.where(first, t1, r2), 0.0)
            lhs = jnp.concatenate([jnp.where(first, t0, 0.0), jnp.where(first, 0.0, second_nope)], axis=1)
            absorbed = nn(lhs.astype(BF16), wk[2 * p : 2 * p + 2].reshape(2 * NOPE, KV))
            parts.append(jnp.concatenate([absorbed, rope], axis=1).reshape(9, 8, WIDE))
        q_all[:, 16 * quad : 16 * quad + 16, :] = jnp.concatenate(parts, axis=1).astype(BF16)

    ask_sib = remote(q_all.at[pl.ds(4 * (1 - c), 4)], q_sib, sib_s.at[0], sib_r.at[0], sib)
    ask_sib.start()
    ask_z = []
    for i in range(1, 4):
        to = (z + i) % 4
        cp = remote(q_all.at[8], q8.at[z], z_s.at[i], z_r.at[i], (g, 2 * to + c))
        cp.start()
        ask_z.append(cp)
    q8[z] = q_all[8]
    ask_sib.wait()

    recent_ok = step_mask(2 * ASK, 16)
    lat_sends = []
    for i in range(4):
        load_kt[i].wait()
        q = jnp.concatenate([q_all[4 * c + i], q_sib[i]], axis=0)[:, 0 : KV + ROPE]
        recent = lat[4 * c + i].astype(BF16)
        s = nn(q, kt[i])
        s_new = jnp.where(recent_ok, nt(q, recent), LOWEST)
        ok = lax.broadcasted_iota(jnp.int32, (1, LRES), 1) < lengths[0, 4 * c + i]
        s = jnp.where(ok, s, LOWEST)
        m = jnp.maximum(jnp.max(s, axis=1, keepdims=True), jnp.max(s_new, axis=1, keepdims=True))
        e = jnp.exp((s - m) * SCALE)
        e_new = jnp.exp((s_new - m) * SCALE)
        total = jnp.sum(e, axis=1, keepdims=True) + jnp.sum(e_new, axis=1, keepdims=True)
        o = nt(e.astype(BF16), kt[i, 0:KV, :]) + nn(e_new.astype(BF16), recent[:, 0:KV])
        o = (o / total).astype(BF16)
        lt[4 * c + i] = o[0:ASK]
        o_sib[i] = o[ASK:]
        cp = remote(o_sib.at[i], lt.at[4 * c + i], sib_s.at[1 + i], sib_r.at[1 + i], sib)
        cp.start()
        lat_sends.append(cp)

    for cp in slice_sends:
        cp.wait()
    keys_sib = remote(k8.at[c], k8.at[c], sib_s.at[5], sib_r.at[5], sib)
    keys_sib.start()
    for cp in ask_z:
        cp.wait()
    keys_sib.wait()
    keys = k8[...].reshape(2 * 16 * TOK, WIDE)
    q = q8[...].reshape(4 * ASK, WIDE)
    flag = (lax.broadcasted_iota(jnp.int32, (8, WIDE), 1) == KV + ROPE).astype(BF16)
    present = nt(flag, keys)[0:1] > 0.5
    s = jnp.where(present, nt(q, keys), LOWEST)
    m = jnp.max(s, axis=1, keepdims=True)
    e = jnp.exp((s - m) * SCALE)
    total = jnp.sum(e, axis=1, keepdims=True)
    o8_send[...] = nn(e.astype(BF16), keys[:, 0:KV]).astype(BF16).reshape(4, ASK, KV)
    left = lax.broadcasted_iota(jnp.int32, (4 * ASK, 128), 1) < 64
    st_send[...] = jnp.where(left, m, total).reshape(4, ASK, 128)
    part_z = []
    for i in range(1, 4):
        to = (z + i) % 4
        cp = remote(o8_send.at[to], o8.at[z], z_s.at[3 + i], z_r.at[3 + i], (g, 2 * to + c))
        cp.start()
        part_z.append(cp)
        cp = remote(st_send.at[to], st8.at[z], z_s.at[6 + i], z_r.at[6 + i], (g, 2 * to + c))
        cp.start()
        part_z.append(cp)
    o8[z] = o8_send[z]
    st8[z] = st_send[z]

    q = q_all[8][:, 0 : KV + ROPE]
    recent = lat[8].astype(BF16)
    s_new = jnp.where(step_mask(ASK, 16), nt(q, recent), LOWEST)
    m_new = jnp.max(s_new, axis=1, keepdims=True)
    e_new = jnp.exp((s_new - m_new) * SCALE)
    total_new = jnp.sum(e_new, axis=1, keepdims=True)
    o_new = nn(e_new.astype(BF16), recent[:, 0:KV])
    for cp in part_z:
        cp.wait()
    m_part = [st8[i][:, 0:1] for i in range(4)]
    m = m_new
    for one in m_part:
        m = jnp.maximum(m, one)
    weight = jnp.exp((m_new - m) * SCALE)
    o = o_new * weight
    total = total_new * weight
    for i in range(4):
        weight = jnp.exp((m_part[i] - m) * SCALE)
        o = o + o8[i].astype(F32) * weight
        total = total + st8[i][:, 64:65] * weight
    lt[8] = (o / total).astype(BF16)
    for cp in lat_sends:
        cp.wait()

    load_wv.wait()
    head_of_row = lax.broadcasted_iota(jnp.int32, (144, 512), 0) % 16 // PAD
    head_of_lane = lax.broadcasted_iota(jnp.int32, (144, 512), 1) // VD
    mine = head_of_row == head_of_lane
    to_row = lax.broadcasted_iota(jnp.int32, (32, 144), 0)
    from_row = lax.broadcasted_iota(jnp.int32, (32, 144), 1)
    picks = (
        (to_row < STEPS * (ROWS + 1))
        & (to_row // STEPS == from_row // 16)
        & (to_row % STEPS == from_row % PAD)
    )
    compact = jnp.where(picks, 1.0, 0.0).astype(BF16)
    for quad in range(4):
        lhs = lt[:, 16 * quad : 16 * quad + 16, :].reshape(144, KV)
        rhs = jnp.concatenate([wv[4 * quad + j] for j in range(4)], axis=1)
        heads_out = jnp.where(mine, nn(lhs, rhs), 0.0).astype(BF16)
        gath[g, :, 512 * quad : 512 * quad + 512] = nn(compact, heads_out).astype(BF16)

    ag_sends = []

    def neighbour(axis, d):
        if axis == 0:
            return (y * 4 + (x + d) % 4, h)
        return ((y + d) % 4 * 4 + x, h)

    def block(k, r1, r2):
        dx, dy = (r1, r2) if k == 0 else (r2, r1)
        return (y + dy) % 4 * 4 + (x + dx) % 4

    def view(k, r1, r2, half):
        rows = pl.ds(0, 32) if half is None else pl.ds(16 * half, 16)
        return gath.at[block(k, r1, r2), rows, pl.ds(1024 * k, 1024)]

    def arrival(k, r1, r2, half):
        return ag_r.at[((k * 4 + r1 % 4) * 4 + r2 % 4) * 2 + (half or 0)]

    def send(k, ring, d, r1, r2, half):
        axis = ring if k == 0 else 1 - ring
        q1, q2 = (r1 - d, r2) if ring == 0 else (r1, r2 - d)
        ref = view(k, r1, r2, half)
        cp = remote(ref, ref, ag_s.at[len(ag_sends)], arrival(k, q1, q2, half), neighbour(axis, d))
        cp.start()
        ag_sends.append(cp)

    def landed(k, r1, r2, half):
        ref = view(k, r1, r2, half)
        remote(ref, ref, ag_s.at[0], arrival(k, r1, r2, half), neighbour(0, 1)).wait_recv()

    for ring in (0, 1):
        for k in (0, 1):
            send(k, ring, 1, 0, 0, None)
            send(k, ring, -1, 0, 0, None)
    for d in (1, -1):
        for k in (0, 1):
            landed(k, -d, 0, None)
            send(k, 0, d, -d, 0, 0 if d == 1 else 1)
            send(k, 1, 1, -d, 0, None)
            send(k, 1, -1, -d, 0, None)
    for k in (0, 1):
        landed(k, 2, 0, 0)
        landed(k, 2, 0, 1)
        send(k, 1, 1, 2, 0, None)
        send(k, 1, -1, 2, 0, None)
    for b in (0, -1, 1, 2):
        for d in (1, -1):
            for k in (0, 1):
                landed(k, b, -d, None)
                send(k, 1, d, b, -d, 0 if d == 1 else 1)
    for b in (0, -1, 1, 2):
        for k in (0, 1):
            landed(k, b, 2, 0)
            landed(k, b, 2, 1)

    load_wo.wait()
    theirs = gath[pl.ds(8 * (1 - c), 8)].reshape(256, 2048)
    p_send[...] = nt(theirs, wo[...]).astype(BF16)
    swap = remote(p_send, p_recv, sib_s.at[6], sib_r.at[6], sib)
    swap.start()
    ours = nt(gath[pl.ds(8 * c, 8)].reshape(256, 2048), wo[...])
    swap.wait()
    p_sum[...] = (ours + p_recv[...].astype(F32)).astype(BF16).reshape(8, 32, 448)

    keeper = g // 2
    slot = (g % 2) * 4 + z
    for i in range(8):
        to = 8 * c + i

        @pl.when(jnp.logical_or(to != g, keeper != h))
        def _():
            remote(p_sum.at[i], red.at[slot], red_s.at[i], red_r.at[slot], (to, keeper)).start()

        @pl.when(jnp.logical_and(to == g, keeper == h))
        def _():
            red[slot] = p_sum[i]

    half_of = g // 8
    for j in range(2):
        for k in range(4):
            at = j * 4 + k

            @pl.when(jnp.logical_or(2 * h + j != g, 2 * k + half_of != h))
            def _():
                remote(p_sum.at[0], red.at[at], red_s.at[0], red_r.at[at], (g, h)).wait_recv()

    for j in range(2):
        acc = red[4 * j].astype(F32)
        for k in range(1, 4):
            acc = acc + red[4 * j + k].astype(F32)
        out[j] = acc.astype(BF16)

    for i in range(8):
        to = 8 * c + i

        @pl.when(jnp.logical_or(to != g, keeper != h))
        def _():
            remote(p_sum.at[i], red.at[slot], red_s.at[i], red_r.at[slot], (to, keeper)).wait_send()

    for cp in ag_sends:
        cp.wait_send()


def body(resident_cache, lengths, slices, placement, queries, latents, w_key, w_value, w_out):
    owners = placement[:, 0]
    count = owners.shape[0]
    alike = owners[:, None] == owners[None, :]
    before = jnp.arange(count)[:, None] < jnp.arange(count)[None, :]
    code = owners * CAP + jnp.sum(alike & before, axis=0).astype(jnp.int32)
    code = jnp.broadcast_to(jnp.repeat(code, TOK)[None, :], (8, count * TOK))
    vmem = pl.BlockSpec(memory_space=pltpu.VMEM)
    smem = pl.BlockSpec(memory_space=pltpu.SMEM)
    anywhere = pl.BlockSpec(memory_space=pl.ANY)
    sems = pltpu.SemaphoreType.DMA
    out = pl.pallas_call(
        kernel,
        out_shape=jax.ShapeDtypeStruct((2, 32, 448), BF16),
        in_specs=[smem, vmem, vmem, vmem] + [anywhere] * 5,
        out_specs=vmem,
        scratch_shapes=[
            pltpu.VMEM((4, KV + ROPE, LRES), BF16),
            pltpu.VMEM((HEADS, NOPE, KV), BF16),
            pltpu.VMEM((HEADS, KV, VD), BF16),
            pltpu.VMEM((448, HEADS * VD), BF16),
            pltpu.VMEM((16, TOK, KV + ROPE), BF16),
            pltpu.VMEM((16 * TOK, WIDE), BF16),
            pltpu.VMEM((16, TOK, WIDE), BF16),
            pltpu.VMEM((ROWS + 1, 8, HEADS * 192), F32),
            pltpu.VMEM((ROWS + 1, 16, KV + ROPE), F32),
            pltpu.VMEM((ROWS + 1, ASK, WIDE), BF16),
            pltpu.VMEM((4, ASK, WIDE), BF16),
            pltpu.VMEM((4, ASK, WIDE), BF16),
            pltpu.VMEM((2, 16 * TOK, WIDE), BF16),
            pltpu.VMEM((4, ASK, KV), BF16),
            pltpu.VMEM((ROWS + 1, ASK, KV), BF16),
            pltpu.VMEM((4, ASK, KV), BF16),
            pltpu.VMEM((4, ASK, KV), BF16),
            pltpu.VMEM((4, ASK, 128), F32),
            pltpu.VMEM((4, ASK, 128), F32),
            pltpu.VMEM((16, 32, 2048), BF16),
            pltpu.VMEM((256, 448), BF16),
            pltpu.VMEM((256, 448), BF16),
            pltpu.VMEM((8, 32, 448), BF16),
            pltpu.VMEM((8, 32, 448), BF16),
            sems((8,)),
            sems((7,)),
            sems((7,)),
            sems((16,)),
            sems((16,)),
            sems((10,)),
            sems((10,)),
            sems((40,)),
            sems((64,)),
            sems((8,)),
            sems((8,)),
        ],
        compiler_params=pltpu.CompilerParams(
            collective_id=0, has_side_effects=True, vmem_limit_bytes=56 * 1024 * 1024
        ),
        name="decode",
    )(
        lengths,
        code,
        jnp.swapaxes(queries[:, 0], 0, 1),
        jnp.swapaxes(latents[:, 0], 0, 1),
        jnp.swapaxes(resident_cache[0], 1, 2),
        slices,
        w_key,
        w_value,
        jnp.swapaxes(w_out, 0, 1),
    )
    mixed = jnp.swapaxes(out, 0, 1).reshape(32, 896)[: STEPS * (ROWS + 1)]
    mixed = jnp.swapaxes(mixed.reshape(ROWS + 1, STEPS, 896), 0, 1)
    return mixed[:, None]


def solution(mesh):
    placed = (
        P("grp", None, None, None),
        P("grp", None),
        P("grp", None, None),
        P("grp", None),
        P(None, "grp", None, "head"),
        P(None, "grp", None, None),
        P("head", None, None),
        P("head", None, None),
        P("head", "grp"),
    )
    return jax.shard_map(
        body, mesh=mesh, in_specs=placed, out_specs=P(None, "grp", None, "head"), check_vma=False
    )
```

time: 273 us -> 61.4 us (0.22)
  waiting for transfers between devices: 164 us -> 0 us
  Pallas kernels: 0 us -> 57 us
  matrix products: 39.6 us -> 0 us
  local copies, waits for them, and re-layouts: 33.6 us -> 2.41 us
  starting transfers between devices: 14.7 us -> 0 us
  between operations: 13.7 us -> 0.01 us
  other arithmetic: 4.4 us -> 1.47 us
    all_gather x1 -> x0, waiting for transfers between devices: 114 us -> none  [body(): lax.all_gather(w_out, 'grp', axis=1, tiled=True)]
    pallas_call x0 -> x1, Pallas kernels: none -> 57 us  [body(): pl.pallas_call(kernel, out_shape=jax.ShapeDtypeStruct((2, 32, 448), BF16)...]
    dot_general x12 -> x0, matrix products: 39.6 us -> none  [the longest x1 14.2 us: body(): jnp.dot(attended, lax.all_gather(w_out, 'grp', axis=1, tiled=True), prefe...]
    unnamed x3 -> x0, waiting for transfers between devices: 30.9 us -> none
    unnamed x18 -> x0, local copies, waits for them, and re-layouts: 21.8 us -> none
    all_to_all x2 -> x0, waiting for transfers between devices: 19.3 us -> none  [the longest x1 19.3 us: body(): lax.all_to_all(packed, 'grp', split_axis=0, concat_axis=0, tiled=True)]
    all_to_all x2 -> x0, starting transfers between devices: 14.5 us -> none  [the longest x1 7.58 us: body(): lax.all_to_all(filled, 'grp', split_axis=0, concat_axis=0, tiled=True)]
    reshape x4 -> x1, local copies, waits for them, and re-layouts: 9.04 us -> 0.75 us  [body(): mixed = jnp.swapaxes(mixed.reshape(ROWS + 1, STEPS, 896), 0, 1)]
  transfers between devices with their start and end apart: 4 -> 0, of which waited for: 3 -> 0; matrix products, arithmetic and copies ran while one was open for 22% -> 0% of each run, Pallas kernels for 0% -> 0%
where the time goes in v1:
time: 61.4 us; the launch traced here: 60.9 us
  Pallas kernels  57 us (93%)
  local copies, waits for them, and re-layouts  2.41 us (4%)
  other arithmetic  1.47 us (2%)
    pallas_call x1, Pallas kernels, body(): pl.pallas_call(kernel, out_shape=jax.ShapeDtypeStruct((2, 32, 448), BF16)...  57 us

profile of v1, /device:TPU:1, one launch (start us, length us, event | category | flops | bytes accessed | tf_op | source)
XLA Modules:
  0.0 60.9 jit_solution(12985564827042833554)
XLA Ops:
  0.0 0.8 %convert_reduce_fusion = s32[16]{0:T(128)S(1)} fusion(s32[16]{0:T(128)} %bitcast.22), kind=kLoop, calls=%fused_computation | loop fusion | flops 1264 | bytes 128 | tf_op jit(solution)/shard_map/reduce_sum | solution.py:343
  0.8 0.7 %multiply_add_fusion = s32[16]{0:T(128)S(1)} fusion(s32[16]{0:T(128)S(1)} %convert_reduce_fusion, s32[16,1]{0,1:T(1,128)} %param.12), kind=kLoop, calls=%fused_computation.3 | loop fusion | flops 32 | bytes 192 | tf_op jit(solution)/shard_map/add | solution.py:343
  1.5 0.1 broadcast_in_dim.15
  1.5 0.1 broadcast_in_dim.16
  1.6 0.6 broadcast_in_dim.17.code
  2.2 57.0 %decode.1 = bf16[2,32,448]{2,1,0:T(8,128)(2,1)} custom-call(s32[1,8]{1,0:T(1,128)} %lengths.1, s32[8,256]{1,0:T(8,128)} %broadcast_in_dim.17.code, bf16[9,3,3072]{2,1,0:T(4,128)(2,1)} %bitcast.20, bf16[9,3,576]{2,1,0:T(4,128)(2,1)} %bitcast.21, bf16[8,576,1536]{2,1,0:T(8,128)(2,1)} %bitcast.17, bf16[16,64,576]{2,1,0:T(8,128)(2,1)} %slices.1, ...), custom_call_target="tpu_custom_call" | custom-call | tf_op jit(solution)/shard_map/decode/pallas_call | solution.py:349
  59.3 0.9 %copy.11 = bf16[27,2,448]{2,1,0:T(2,128)(2,1)S(1)} copy(bf16[27,2,448]{2,0,1:T(8,128)(2,1)} %bitcast.19) | data formatting | bytes 96768 | tf_op jit(solution)/shard_map/slice | solution.py:406
  60.2 0.8 %reshape.8 = bf16[9,3,896]{2,1,0:T(4,128)(2,1)} reshape(bf16[27,2,448]{2,1,0:T(2,128)(2,1)S(1)} %copy.11) | data formatting | bytes 96768 | tf_op jit(solution)/shard_map/reshape | solution.py:407

commit v2 on v1

v2 whole, which is shorter than its diff:
```python
import math

import jax
import jax.numpy as jnp
from jax import lax
from jax.experimental import pallas as pl
from jax.experimental.pallas import tpu as pltpu
from jax.sharding import PartitionSpec as P

KV = 512
ROPE = 64
NOPE = 128
VD = 128
ROWS = 8
LRES = 1536
SL = 64
CAP = 2
STEPS = 3

MESH = pl.DeviceIdType.MESH
SCALE = 1.0 / math.sqrt(NOPE + ROPE)
LOWEST = -3.0e38
BF16 = jnp.bfloat16
F32 = jnp.float32
WIDE = 640
PAD = 4
HEADS = 16
ASK = HEADS * PAD
TOK = 16


def remote(src, dst, send_sem, recv_sem, dev):
    return pltpu.make_async_remote_copy(
        src_ref=src, dst_ref=dst, send_sem=send_sem, recv_sem=recv_sem, device_id=dev, device_id_type=MESH
    )


def nt(a, b):
    return lax.dot_general(a, b, (((1,), (1,)), ((), ())), preferred_element_type=F32)


def nn(a, b):
    return jnp.dot(a, b, preferred_element_type=F32)


def step_mask(rows, width):
    step = lax.broadcasted_iota(jnp.int32, (rows, width), 0) % PAD
    at = lax.broadcasted_iota(jnp.int32, (rows, width), 1)
    return (at < STEPS) & (at <= step)


def kernel(
    lengths, placement, queries, latents, cache, slices, w_key, w_value, w_out,
    out,
    kt, wk, wv, wo, sl, slw, k_send, qv, lv, qf, lat,
    q_all, q_sib, q8, k8, o_sib, lt, o8_send, o8,
    gath, p_all, p_send, p_recv, p_sum, red,
    dma, sib_s, sib_r, sl_s, sl_r, z_s, z_r, ag_s, ag_r, red_s, red_r,
):
    g = lax.axis_index("grp")
    h = lax.axis_index("head")
    y, x = g // 4, g % 4
    z, c = h // 2, h % 2
    sib = (g, h + 1 - 2 * c)

    load_sl = pltpu.make_async_copy(slices.at[:, pl.ds(TOK * z, TOK), :], sl, dma.at[1])
    load_qv = pltpu.make_async_copy(queries, qv, dma.at[8])
    load_lv = pltpu.make_async_copy(latents, lv, dma.at[9])
    load_wk = pltpu.make_async_copy(w_key, wk, dma.at[0])
    load_kt = [pltpu.make_async_copy(cache.at[4 * c + i], kt.at[i], dma.at[2 + i]) for i in range(4)]
    load_wv = pltpu.make_async_copy(w_value, wv, dma.at[6])
    load_wo = pltpu.make_async_copy(w_out, wo.at[0:448], dma.at[7])
    load_qv.start()
    load_sl.start()
    load_wk.start()
    load_lv.start()
    load_kt[0].start()
    load_kt[1].start()
    load_wv.start()
    load_kt[2].start()
    load_kt[3].start()
    load_wo.start()

    barrier = pltpu.get_barrier_semaphore()
    for i in range(1, 16):
        pl.semaphore_signal(barrier, inc=1, device_id=((g + i) % 16, h), device_id_type=MESH)
    for i in range(1, 8):
        pl.semaphore_signal(barrier, inc=1, device_id=(g, (h + i) % 8), device_id_type=MESH)

    qf[...] = jnp.zeros_like(qf)
    lat[...] = jnp.zeros_like(lat)
    owners = [placement[0, i] for i in range(16)]
    owner_of_lane = lax.broadcasted_iota(jnp.int32, (8, 16 * TOK), 1) // TOK
    code = jnp.zeros((8, 16 * TOK), jnp.int32)
    for i in range(16):
        rank = jnp.int32(0)
        for j in range(i):
            rank = rank + jnp.where(owners[j] == owners[i], 1, 0)
        code = jnp.where(owner_of_lane == i, owners[i] * CAP + rank, code)

    slw[:, KV:WIDE] = jnp.ones((16 * TOK, WIDE - KV), BF16)
    at0 = lax.broadcasted_iota(jnp.int32, (16 * TOK, 16 * TOK), 0)
    at1 = lax.broadcasted_iota(jnp.int32, (16 * TOK, 16 * TOK), 1)
    chosen = (at0 % TOK == at1 % TOK) & ((at0 // TOK) * CAP + c == code[0:1, :])
    selector = jnp.where(chosen, 1.0, 0.0).astype(BF16)
    load_sl.wait()
    slw[:, 0 : KV + ROPE] = sl[...].reshape(16 * TOK, KV + ROPE)
    k_send[...] = nn(selector, slw[...]).astype(BF16).reshape(16, TOK, WIDE)

    load_qv.wait()
    load_lv.wait()
    for r in range(ROWS + 1):
        v = qv[r].astype(F32)
        qf[r, 0:STEPS, :] = v
        qf[r, PAD : PAD + STEPS, :] = v
        lat[r, 0:STEPS, :] = lv[r].astype(F32)

    pl.semaphore_wait(barrier, 22)

    slice_sends = []
    for i in range(1, 16):
        to = (g + i) % 16
        cp = remote(k_send.at[to], k8.at[c, pl.ds(TOK * g, TOK)], sl_s.at[i], sl_r.at[i], (to, h))
        cp.start()
        slice_sends.append(cp)
    k8[c, pl.ds(TOK * g, TOK), :] = k_send[g]

    load_wk.wait()
    row = lax.broadcasted_iota(jnp.int32, (72, 128), 0)
    lane = lax.broadcasted_iota(jnp.int32, (72, 128), 1)
    first = row % 8 < PAD
    low = lane < ROPE
    for quad in range(4):
        parts = []
        for p in (2 * quad, 2 * quad + 1):
            t = qf[:, :, 384 * p : 384 * p + 384].reshape(72, 384)
            t0, t1, t2 = t[:, 0:128], t[:, 128:256], t[:, 256:384]
            r1, r2 = pltpu.roll(t1, 64, 1), pltpu.roll(t2, 64, 1)
            second_nope = jnp.where(low, r1, r2)
            rope = jnp.where(low, jnp.where(first, t1, r2), 0.0)
            lhs = jnp.concatenate([jnp.where(first, t0, 0.0), jnp.where(first, 0.0, second_nope)], axis=1)
            absorbed = nn(lhs.astype(BF16), wk[2 * p : 2 * p + 2].reshape(2 * NOPE, KV))
            parts.append(jnp.concatenate([absorbed, rope], axis=1).reshape(9, 8, WIDE))
        q_all[:, 16 * quad : 16 * quad + 16, :] = jnp.concatenate(parts, axis=1).astype(BF16)

    ask_sib = remote(q_all.at[pl.ds(4 * (1 - c), 4)], q_sib, sib_s.at[0], sib_r.at[0], sib)
    ask_sib.start()
    ask_z = []
    for i in range(1, 4):
        to = (z + i) % 4
        cp = remote(q_all.at[8], q8.at[z], z_s.at[i], z_r.at[i], (g, 2 * to + c))
        cp.start()
        ask_z.append(cp)
    q8[z] = q_all[8]
    ask_sib.wait()

    recent_ok = step_mask(2 * ASK, 16)

    def resident(i):
        load_kt[i].wait()
        q = jnp.concatenate([q_all[4 * c + i], q_sib[i]], axis=0)[:, 0 : KV + ROPE]
        recent = lat[4 * c + i].astype(BF16)
        s = nn(q, kt[i])
        s_new = jnp.where(recent_ok, nt(q, recent), LOWEST)
        ok = lax.broadcasted_iota(jnp.int32, (1, LRES), 1) < lengths[0, 4 * c + i]
        s = jnp.where(ok, s, LOWEST)
        m = jnp.maximum(jnp.max(s, axis=1, keepdims=True), jnp.max(s_new, axis=1, keepdims=True))
        e = jnp.exp((s - m) * SCALE)
        e_new = jnp.exp((s_new - m) * SCALE)
        total = jnp.sum(e, axis=1, keepdims=True) + jnp.sum(e_new, axis=1, keepdims=True)
        o = nt(e.astype(BF16), kt[i, 0:KV, :]) + nn(e_new.astype(BF16), recent[:, 0:KV])
        o = (o / total).astype(BF16)
        at = (i // 2) * 4 + c * 2 + i % 2
        lt[at] = o[0:ASK]
        o_sib[i] = o[ASK:]
        cp = remote(o_sib.at[i], lt.at[at], sib_s.at[1 + i], sib_r.at[1 + i], sib)
        cp.start()
        return cp

    def values(part):
        lo, count = (0, 4) if part == 0 else (4, 5)
        rows = 16 * count
        head_of_row = lax.broadcasted_iota(jnp.int32, (rows, 512), 0) % 16 // PAD
        head_of_lane = lax.broadcasted_iota(jnp.int32, (rows, 512), 1) // VD
        mine = head_of_row == head_of_lane
        to_row = lax.broadcasted_iota(jnp.int32, (16, rows), 0)
        from_row = lax.broadcasted_iota(jnp.int32, (16, rows), 1)
        picks = (
            (to_row < STEPS * count)
            & (to_row // STEPS == from_row // 16)
            & (to_row % STEPS == from_row % PAD)
        )
        compact = jnp.where(picks, 1.0, 0.0).astype(BF16)
        for quad in range(4):
            lhs = lt[lo : lo + count, 16 * quad : 16 * quad + 16, :].reshape(rows, KV)
            rhs = jnp.concatenate([wv[4 * quad + j] for j in range(4)], axis=1)
            heads_out = jnp.where(mine, nn(lhs, rhs), 0.0).astype(BF16)
            gath[part, g, :, 512 * quad : 512 * quad + 512] = nn(compact, heads_out).astype(BF16)

    ag_sends = []

    def neighbour(axis, d):
        if axis == 0:
            return (y * 4 + (x + d) % 4, h)
        return ((y + d) % 4 * 4 + x, h)

    def view(part, k, r1, r2, half):
        dx, dy = (r1, r2) if k == 0 else (r2, r1)
        columns = pl.ds(1024 * k, 1024) if half is None else pl.ds(1024 * k + 512 * half, 512)
        return gath.at[part, (y + dy) % 4 * 4 + (x + dx) % 4, :, columns]

    def arrival(part, k, r1, r2, half):
        return ag_r.at[(((part * 2 + k) * 4 + r1 % 4) * 4 + r2 % 4) * 2 + (half or 0)]

    def send(part, k, ring, d, r1, r2, half):
        axis = ring if k == 0 else 1 - ring
        q1, q2 = (r1 - d, r2) if ring == 0 else (r1, r2 - d)
        ref = view(part, k, r1, r2, half)
        cp = remote(ref, ref, ag_s.at[len(ag_sends)], arrival(part, k, q1, q2, half), neighbour(axis, d))
        cp.start()
        ag_sends.append(cp)

    def landed(part, k, r1, r2, half):
        ref = view(part, k, r1, r2, half)
        remote(ref, ref, ag_s.at[0], arrival(part, k, r1, r2, half), neighbour(0, 1)).wait_recv()

    def gather_own(part):
        for ring in (0, 1):
            for k in (0, 1):
                send(part, k, ring, 1, 0, 0, None)
                send(part, k, ring, -1, 0, 0, None)

    def gather_near(part):
        for d in (1, -1):
            for k in (0, 1):
                landed(part, k, -d, 0, None)
                send(part, k, 0, d, -d, 0, 0 if d == 1 else 1)
                send(part, k, 1, 1, -d, 0, None)
                send(part, k, 1, -1, -d, 0, None)

    def gather_far(part):
        for k in (0, 1):
            landed(part, k, 2, 0, 0)
            landed(part, k, 2, 0, 1)
            send(part, k, 1, 1, 2, 0, None)
            send(part, k, 1, -1, 2, 0, None)

    def gather_relay(part):
        for b in (0, -1, 1, 2):
            for d in (1, -1):
                for k in (0, 1):
                    landed(part, k, b, -d, None)
                    send(part, k, 1, d, b, -d, 0 if d == 1 else 1)

    def gather_end(part):
        for b in (0, -1, 1, 2):
            for k in (0, 1):
                landed(part, k, b, 2, 0)
                landed(part, k, b, 2, 1)

    def project(part):
        p_all[...] = nt(gath[part].reshape(256, 2048), wo[...]).reshape(16, 16, 512)
        p_send[part] = p_all[pl.ds(8 * (1 - c), 8)].astype(BF16)
        cp = remote(p_send.at[part], p_recv.at[part], sib_s.at[6 + part], sib_r.at[6 + part], sib)
        cp.start()
        cp.wait()
        p_sum[part] = (p_all[pl.ds(8 * c, 8)] + p_recv[part].astype(F32)).astype(BF16)

    keeper = g // 2
    slot = (g % 2) * 4 + z

    def hand(part, i):
        return remote(
            p_sum.at[part, i], red.at[part, slot], red_s.at[8 * part + i], red_r.at[8 * part + slot],
            (8 * c + i, keeper),
        )

    def hand_out(part):
        for i in range(8):
            to = 8 * c + i

            @pl.when(jnp.logical_or(to != g, keeper != h))
            def _():
                hand(part, i).start()

            @pl.when(jnp.logical_and(to == g, keeper == h))
            def _():
                red[part, slot] = p_sum[part, i]

    def take_in(part):
        half_of = g // 8
        for j in range(2):
            for k in range(4):
                at = j * 4 + k

                @pl.when(jnp.logical_or(2 * h + j != g, 2 * k + half_of != h))
                def _():
                    remote(
                        p_sum.at[part, 0], red.at[part, at], red_s.at[0], red_r.at[8 * part + at], sib
                    ).wait_recv()

        sums = []
        for j in range(2):
            acc = red[part, 4 * j].astype(F32)
            for k in range(1, 4):
                acc = acc + red[part, 4 * j + k].astype(F32)
            sums.append(acc)
        shifted = pltpu.roll(sums[1], 64, 1)
        lane = lax.broadcasted_iota(jnp.int32, (16, 128), 1)
        middle = jnp.where(lane < 64, sums[0][:, 384:512], shifted[:, 0:128])
        mixed = jnp.concatenate([sums[0][:, 0:384], middle, shifted[:, 128:512]], axis=1)
        rows = (0, 1, 4, 5) if part == 0 else (2, 3, 6, 7, 8)
        for a, r in enumerate(rows):
            out[r] = mixed[STEPS * a : STEPS * a + STEPS].astype(BF16)

    wo[448:512, :] = jnp.zeros((64, 2048), BF16)
    lat_sends = [resident(0), resident(1)]
    for cp in lat_sends:
        cp.wait()
    load_wv.wait()
    values(0)
    gather_own(0)
    lat_sends = [resident(2)]
    gather_near(0)

    for cp in slice_sends:
        cp.wait()
    keys_sib = remote(k8.at[c], k8.at[c], sib_s.at[5], sib_r.at[5], sib)
    keys_sib.start()
    lat_sends.append(resident(3))
    gather_far(0)

    for cp in ask_z:
        cp.wait()
    keys_sib.wait()
    keys = k8[...].reshape(2 * 16 * TOK, WIDE)
    q = q8[...].reshape(4 * ASK, WIDE)
    flag = (lax.broadcasted_iota(jnp.int32, (8, WIDE), 1) == KV + ROPE).astype(BF16)
    present = nt(flag, keys)[0:1] > 0.5
    s = jnp.where(present, nt(q, keys), LOWEST)
    m = jnp.max(s, axis=1, keepdims=True)
    e = jnp.exp((s - m) * SCALE)
    total = jnp.sum(e, axis=1, keepdims=True)
    o = nn(e.astype(BF16), keys[:, 0:KV])
    lane = lax.broadcasted_iota(jnp.int32, (4 * ASK, 128), 1)
    stats = jnp.zeros((4 * ASK, 128), F32)
    for n, rest in enumerate((m, total)):
        for t in range(3):
            piece = rest.astype(BF16).astype(F32)
            rest = rest - piece
            stats = jnp.where(lane == 3 * n + t, piece, stats)
    o8_send[...] = jnp.concatenate([o, stats], axis=1).astype(BF16).reshape(4, ASK, WIDE)
    part_z = []
    for i in range(1, 4):
        to = (z + i) % 4
        cp = remote(o8_send.at[to], o8.at[z], z_s.at[3 + i], z_r.at[3 + i], (g, 2 * to + c))
        cp.start()
        part_z.append(cp)
    o8[z] = o8_send[z]

    gather_relay(0)

    q = q_all[8][:, 0 : KV + ROPE]
    recent = lat[8].astype(BF16)
    s_new = jnp.where(step_mask(ASK, 16), nt(q, recent), LOWEST)
    m_new = jnp.max(s_new, axis=1, keepdims=True)
    e_new = jnp.exp((s_new - m_new) * SCALE)
    total_new = jnp.sum(e_new, axis=1, keepdims=True)
    o_new = nn(e_new.astype(BF16), recent[:, 0:KV])
    for cp in part_z:
        cp.wait()
    m_part, total_part = [], []
    for i in range(4):
        st = o8[i][:, KV:WIDE].astype(F32)
        m_part.append(st[:, 0:1] + st[:, 1:2] + st[:, 2:3])
        total_part.append(st[:, 3:4] + st[:, 4:5] + st[:, 5:6])
    m = m_new
    for one in m_part:
        m = jnp.maximum(m, one)
    weight = jnp.exp((m_new - m) * SCALE)
    o = o_new * weight
    total = total_new * weight
    for i in range(4):
        weight = jnp.exp((m_part[i] - m) * SCALE)
        o = o + o8[i][:, 0:KV].astype(F32) * weight
        total = total + total_part[i] * weight
    lt[8] = (o / total).astype(BF16)
    for cp in lat_sends:
        cp.wait()
    values(1)
    gather_own(1)

    load_wo.wait()
    gather_end(0)
    project(0)
    gather_near(1)
    hand_out(0)
    gather_far(1)
    gather_relay(1)
    take_in(0)
    gather_end(1)
    project(1)
    hand_out(1)
    take_in(1)

    for part in (0, 1):
        for i in range(8):
            pl.when(jnp.logical_or(8 * c + i != g, keeper != h))(hand(part, i).wait_send)
    for cp in ag_sends:
        cp.wait_send()


def body(resident_cache, lengths, slices, placement, queries, latents, w_key, w_value, w_out):
    vmem = pl.BlockSpec(memory_space=pltpu.VMEM)
    smem = pl.BlockSpec(memory_space=pltpu.SMEM)
    anywhere = pl.BlockSpec(memory_space=pl.ANY)
    sems = pltpu.SemaphoreType.DMA
    out = pl.pallas_call(
        kernel,
        out_shape=jax.ShapeDtypeStruct((ROWS + 1, STEPS, 896), BF16),
        in_specs=[smem, smem] + [anywhere] * 7,
        out_specs=vmem,
        scratch_shapes=[
            pltpu.VMEM((4, KV + ROPE, LRES), BF16),
            pltpu.VMEM((HEADS, NOPE, KV), BF16),
            pltpu.VMEM((HEADS, KV, VD), BF16),
            pltpu.VMEM((512, HEADS * VD), BF16),
            pltpu.VMEM((16, TOK, KV + ROPE), BF16),
            pltpu.VMEM((16 * TOK, WIDE), BF16),
            pltpu.VMEM((16, TOK, WIDE), BF16),
            pltpu.VMEM((ROWS + 1, STEPS, HEADS * 192), BF16),
            pltpu.VMEM((ROWS + 1, STEPS, KV + ROPE), BF16),
            pltpu.VMEM((ROWS + 1, 8, HEADS * 192), F32),
            pltpu.VMEM((ROWS + 1, 16, KV + ROPE), F32),
            pltpu.VMEM((ROWS + 1, ASK, WIDE), BF16),
            pltpu.VMEM((4, ASK, WIDE), BF16),
            pltpu.VMEM((4, ASK, WIDE), BF16),
            pltpu.VMEM((2, 16 * TOK, WIDE), BF16),
            pltpu.VMEM((4, ASK, KV), BF16),
            pltpu.VMEM((ROWS + 1, ASK, KV), BF16),
            pltpu.VMEM((4, ASK, WIDE), BF16),
            pltpu.VMEM((4, ASK, WIDE), BF16),
            pltpu.VMEM((2, 16, 16, 2048), BF16),
            pltpu.VMEM((16, 16, 512), F32),
            pltpu.VMEM((2, 8, 16, 512), BF16),
            pltpu.VMEM((2, 8, 16, 512), BF16),
            pltpu.VMEM((2, 8, 16, 512), BF16),
            pltpu.VMEM((2, 8, 16, 512), BF16),
            sems((10,)),
            sems((8,)),
            sems((8,)),
            sems((16,)),
            sems((16,)),
            sems((7,)),
            sems((7,)),
            sems((80,)),
            sems((128,)),
            sems((16,)),
            sems((16,)),
        ],
        compiler_params=pltpu.CompilerParams(
            collective_id=0, has_side_effects=True, vmem_limit_bytes=56 * 1024 * 1024
        ),
        name="decode",
    )(
        lengths,
        placement.reshape(1, 16),
        jnp.swapaxes(queries[:, 0], 0, 1),
        jnp.swapaxes(latents[:, 0], 0, 1),
        jnp.swapaxes(resident_cache[0], 1, 2),
        slices,
        w_key,
        w_value,
        jnp.swapaxes(w_out, 0, 1),
    )
    return jnp.swapaxes(out, 0, 1)[:, None]


def solution(mesh):
    placed = (
        P("grp", None, None, None),
        P("grp", None),
        P("grp", None, None),
        P("grp", None),
        P(None, "grp", None, "head"),
        P(None, "grp", None, None),
        P("head", None, None),
        P("head", None, None),
        P("head", "grp"),
    )
    return jax.shard_map(
        body, mesh=mesh, in_specs=placed, out_specs=P(None, "grp", None, "head"), check_vma=False
    )
```

time: 61.4 us -> 58.4 us (0.951)
  other arithmetic: 1.47 us -> 0 us
  local copies, waits for them, and re-layouts: 2.41 us -> 1.49 us
    unnamed x0 -> x1, local copies, waits for them, and re-layouts: none -> 1.49 us
    slice x1 -> x0, local copies, waits for them, and re-layouts: 0.9 us -> none  [body(): mixed = jnp.swapaxes(out, 0, 1).reshape(32, 896)[:STEPS * (ROWS + 1)]]
    reduce_sum x1 -> x0, other arithmetic: 0.82 us -> none  [body(): code = owners * CAP + jnp.sum(alike & before, axis=0).astype(jnp.int32)]
    broadcast_in_dim x3 -> x0, local copies, waits for them, and re-layouts: 0.76 us -> none  [body(): code = jnp.broadcast_to(jnp.repeat(code, TOK)[None, :], (8, count * TOK))]
    reshape x1 -> x0, local copies, waits for them, and re-layouts: 0.75 us -> none  [body(): mixed = jnp.swapaxes(mixed.reshape(ROWS + 1, STEPS, 896), 0, 1)]
    add x1 -> x0, other arithmetic: 0.66 us -> none  [body(): code = owners * CAP + jnp.sum(alike & before, axis=0).astype(jnp.int32)]
where the time goes in v2:
time: 58.4 us; the launch traced here: 58.2 us
  Pallas kernels  56.7 us (97%)
  local copies, waits for them, and re-layouts  1.49 us (3%)
    pallas_call x1, Pallas kernels, body(): pl.pallas_call(kernel, out_shape=jax.ShapeDtypeStruct((ROWS + 1, STEPS, 8...  56.7 us
    unnamed x1, local copies, waits for them, and re-layouts  1.49 us

profile of v2, /device:TPU:1, one launch (start us, length us, event | category | flops | bytes accessed | tf_op | source)
XLA Modules:
  0.0 58.2 jit_solution(9891620359282018558)
XLA Ops:
  0.0 56.7 %decode.1 = bf16[9,3,896]{2,1,0:T(4,128)(2,1)} custom-call(s32[1,8]{1,0:T(1,128)} %lengths.1, s32[1,16]{1,0:T(1,128)} %bitcast.19, bf16[9,3,3072]{2,1,0:T(4,128)(2,1)} %bitcast.17, bf16[9,3,576]{2,1,0:T(4,128)(2,1)} %bitcast.18, bf16[8,576,1536]{2,1,0:T(8,128)(2,1)} %bitcast.14, bf16[16,64,576]{2,1,0:T(8,128)(2,1)} %slices.1, bf16[16,128,512]{2,1,0:T(8,128)(2,1)} %w_key.1, ...), custom_call_target="tpu_custom_call" | custom-call | tf_op jit(solution)/shard_map/decode/pallas_call | solution.py:418
  56.7 1.5 %copy.11 = bf16[3,1,9,896]{3,0,2,1:T(4,128)(2,1)} copy(bf16[3,1,9,896]{3,0,2,1:T(4,128)(2,1)} %bitcast.16) | data formatting | bytes 96768

commit v3 on v2

--- a/solution.py
+++ b/solution.py
@@ -26,6 +26,7 @@
 PAD = 4
 HEADS = 16
 ASK = HEADS * PAD
+WIDTH = (768, 1024)
 TOK = 16
 
 
@@ -54,7 +55,7 @@
     out,
     kt, wk, wv, wo, sl, slw, k_send, qv, lv, qf, lat,
     q_all, q_sib, q8, k8, o_sib, lt, o8_send, o8,
-    gath, p_all, p_send, p_recv, p_sum, red,
+    gath_a, gath_b, unpack, p_all, p_send, p_recv, p_sum, red,
     dma, sib_s, sib_r, sl_s, sl_r, z_s, z_r, ag_s, ag_r, red_s, red_r,
 ):
     g = lax.axis_index("grp")
@@ -62,6 +63,7 @@
     y, x = g // 4, g % 4
     z, c = h // 2, h % 2
     sib = (g, h + 1 - 2 * c)
+    gath = (gath_a, gath_b)
 
     load_sl = pltpu.make_async_copy(slices.at[:, pl.ds(TOK * z, TOK), :], sl, dma.at[1])
     load_qv = pltpu.make_async_copy(queries, qv, dma.at[8])
@@ -97,6 +99,13 @@
         for j in range(i):
             rank = rank + jnp.where(owners[j] == owners[i], 1, 0)
         code = jnp.where(owner_of_lane == i, owners[i] * CAP + rank, code)
+
+    wo[448:512, :] = jnp.zeros((64, 2048), BF16)
+    to_row = lax.broadcasted_iota(jnp.int32, (256, 256), 0)
+    from_row = lax.broadcasted_iota(jnp.int32, (256, 256), 1)
+    for b in range(3):
+        back = (to_row // 16 == from_row // 16) & (to_row % 16 == from_row % 16 - 12 + 4 * b) & (from_row % 16 >= 12)
+        unpack[:, 256 * b : 256 * b + 256] = jnp.where(back, 1.0, 0.0).astype(BF16)
 
     slw[:, KV:WIDE] = jnp.ones((16 * TOK, WIDE - KV), BF16)
     at0 = lax.broadcasted_iota(jnp.int32, (16 * TOK, 16 * TOK), 0)
@@ -183,88 +192,78 @@
         head_of_row = lax.broadcasted_iota(jnp.int32, (rows, 512), 0) % 16 // PAD
         head_of_lane = lax.broadcasted_iota(jnp.int32, (rows, 512), 1) // VD
         mine = head_of_row == head_of_lane
-        to_row = lax.broadcasted_iota(jnp.int32, (16, rows), 0)
-        from_row = lax.broadcasted_iota(jnp.int32, (16, rows), 1)
-        picks = (
-            (to_row < STEPS * count)
-            & (to_row // STEPS == from_row // 16)
-            & (to_row % STEPS == from_row % PAD)
-        )
-        compact = jnp.where(picks, 1.0, 0.0).astype(BF16)
+        heads_out = []
         for quad in range(4):
             lhs = lt[lo : lo + count, 16 * quad : 16 * quad + 16, :].reshape(rows, KV)
             rhs = jnp.concatenate([wv[4 * quad + j] for j in range(4)], axis=1)
-            heads_out = jnp.where(mine, nn(lhs, rhs), 0.0).astype(BF16)
-            gath[part, g, :, 512 * quad : 512 * quad + 512] = nn(compact, heads_out).astype(BF16)
+            heads_out.append(jnp.where(mine, nn(lhs, rhs), 0.0).astype(BF16))
+        to_row = lax.broadcasted_iota(jnp.int32, (16, rows), 0)
+        from_row = lax.broadcasted_iota(jnp.int32, (16, rows), 1)
+
+        def picks(at):
+            return (at // STEPS == from_row // 16) & (at % STEPS == from_row % PAD)
+
+        blocks = []
+        if part == 0:
+            direct = jnp.where((to_row < 12) & picks(to_row), 1.0, 0.0).astype(BF16)
+            for b in range(3):
+                under = jnp.where((to_row >= 12) & picks(4 * b + to_row - 12), 1.0, 0.0).astype(BF16)
+                blocks.append(nn(direct, heads_out[b]) + nn(under, heads_out[3]))
+        else:
+            direct = jnp.where((to_row < 15) & picks(to_row), 1.0, 0.0).astype(BF16)
+            for b in range(4):
+                blocks.append(nn(direct, heads_out[b]))
+        block = jnp.concatenate(blocks, axis=1).astype(BF16)
+        half = WIDTH[part]
+        gath[part][0, 4 * y + x] = block[:, 0:half]
+        gath[part][1, 4 * x + y] = block[:, half:]
 
     ag_sends = []
 
-    def neighbour(axis, d):
+    def along(axis, d):
         if axis == 0:
-            return (y * 4 + (x + d) % 4, h)
+            return (4 * y + (x + d) % 4, h)
         return ((y + d) % 4 * 4 + x, h)
 
-    def view(part, k, r1, r2, half):
-        dx, dy = (r1, r2) if k == 0 else (r2, r1)
-        columns = pl.ds(1024 * k, 1024) if half is None else pl.ds(1024 * k + 512 * half, 512)
-        return gath.at[part, (y + dy) % 4 * 4 + (x + dx) % 4, :, columns]
-
-    def arrival(part, k, r1, r2, half):
-        return ag_r.at[(((part * 2 + k) * 4 + r1 % 4) * 4 + r2 % 4) * 2 + (half or 0)]
-
-    def send(part, k, ring, d, r1, r2, half):
-        axis = ring if k == 0 else 1 - ring
-        q1, q2 = (r1 - d, r2) if ring == 0 else (r1, r2 - d)
-        ref = view(part, k, r1, r2, half)
-        cp = remote(ref, ref, ag_s.at[len(ag_sends)], arrival(part, k, q1, q2, half), neighbour(axis, d))
-        cp.start()
-        ag_sends.append(cp)
-
-    def landed(part, k, r1, r2, half):
-        ref = view(part, k, r1, r2, half)
-        remote(ref, ref, ag_s.at[0], arrival(part, k, r1, r2, half), neighbour(0, 1)).wait_recv()
-
-    def gather_own(part):
-        for ring in (0, 1):
-            for k in (0, 1):
-                send(part, k, ring, 1, 0, 0, None)
-                send(part, k, ring, -1, 0, 0, None)
-
-    def gather_near(part):
-        for d in (1, -1):
-            for k in (0, 1):
-                landed(part, k, -d, 0, None)
-                send(part, k, 0, d, -d, 0, 0 if d == 1 else 1)
-                send(part, k, 1, 1, -d, 0, None)
-                send(part, k, 1, -1, -d, 0, None)
-
-    def gather_far(part):
+    def blocks_of(part, k, ring, d):
+        one, two = (x, y) if k == 0 else (y, x)
+        if ring == 0:
+            return gath[part].at[k, pl.ds(4 * two + (one - d) % 4, 1)]
+        return gath[part].at[k, pl.ds(4 * ((two - d) % 4), 4)]
+
+    def gather_send(part, ring):
         for k in (0, 1):
-            landed(part, k, 2, 0, 0)
-            landed(part, k, 2, 0, 1)
-            send(part, k, 1, 1, 2, 0, None)
-            send(part, k, 1, -1, 2, 0, None)
-
-    def gather_relay(part):
-        for b in (0, -1, 1, 2):
-            for d in (1, -1):
-                for k in (0, 1):
-                    landed(part, k, b, -d, None)
-                    send(part, k, 1, d, b, -d, 0 if d == 1 else 1)
-
-    def gather_end(part):
-        for b in (0, -1, 1, 2):
-            for k in (0, 1):
-                landed(part, k, b, 2, 0)
-                landed(part, k, b, 2, 1)
+            ref = blocks_of(part, k, ring, 0)
+            for d in (2, 1, 3):
+                n = ((part * 2 + k) * 2 + ring) * 4 + d
+                cp = remote(ref, ref, ag_s.at[n], ag_r.at[n], along(ring if k == 0 else 1 - ring, d))
+                cp.start()
+                ag_sends.append(cp)
+
+    def gather_wait(part, ring):
+        for k in (0, 1):
+            for d in (1, 3, 2):
+                n = ((part * 2 + k) * 2 + ring) * 4 + d
+                ref = blocks_of(part, k, ring, d)
+                remote(ref, ref, ag_s.at[n], ag_r.at[n], along(ring if k == 0 else 1 - ring, d)).wait_recv()
 
     def project(part):
-        p_all[...] = nt(gath[part].reshape(256, 2048), wo[...]).reshape(16, 16, 512)
-        p_send[part] = p_all[pl.ds(8 * (1 - c), 8)].astype(BF16)
+        half = WIDTH[part]
+        first_half = gath[part][0].reshape(256, half)
+        second_half = jnp.concatenate([gath[part][1, 4 * (i % 4) + i // 4] for i in range(16)], axis=0)
+        lhs = jnp.concatenate([first_half, second_half], axis=1)
+        if part == 0:
+            tall = jnp.concatenate([lhs[:, 512 * b : 512 * b + 512] for b in range(3)], axis=0)
+            lhs = jnp.concatenate([lhs, nn(unpack[...], tall).astype(BF16)], axis=1)
+        p_all[part] = nt(lhs, wo[...]).reshape(16, 16, 512)
+        p_send[part] = p_all[part, pl.ds(8 * (1 - c), 8)].astype(BF16)
         cp = remote(p_send.at[part], p_recv.at[part], sib_s.at[6 + part], sib_r.at[6 + part], sib)
         cp.start()
-        cp.wait()
-        p_sum[part] = (p_all[pl.ds(8 * c, 8)] + p_recv[part].astype(F32)).astype(BF16)
+        return cp
+
+    def add_cores(part, cp):
+        cp.wait()
+        p_sum[part] = (p_all[part, pl.ds(8 * c, 8)] + p_recv[part].astype(F32)).astype(BF16)
 
     keeper = g // 2
     slot = (g % 2) * 4 + z
@@ -313,22 +312,20 @@
         for a, r in enumerate(rows):
             out[r] = mixed[STEPS * a : STEPS * a + STEPS].astype(BF16)
 
-    wo[448:512, :] = jnp.zeros((64, 2048), BF16)
     lat_sends = [resident(0), resident(1)]
     for cp in lat_sends:
         cp.wait()
     load_wv.wait()
     values(0)
-    gather_own(0)
-    lat_sends = [resident(2)]
-    gather_near(0)
+    gather_send(0, 0)
 
     for cp in slice_sends:
         cp.wait()
     keys_sib = remote(k8.at[c], k8.at[c], sib_s.at[5], sib_r.at[5], sib)
     keys_sib.start()
-    lat_sends.append(resident(3))
-    gather_far(0)
+    lat_sends = [resident(2)]
+    gather_wait(0, 0)
+    gather_send(0, 1)
 
     for cp in ask_z:
         cp.wait()
@@ -358,7 +355,7 @@
         part_z.append(cp)
     o8[z] = o8_send[z]
 
-    gather_relay(0)
+    lat_sends.append(resident(3))
 
     q = q_all[8][:, 0 : KV + ROPE]
     recent = lat[8].astype(BF16)
@@ -388,18 +385,19 @@
     for cp in lat_sends:
         cp.wait()
     values(1)
-    gather_own(1)
+    gather_send(1, 0)
 
     load_wo.wait()
-    gather_end(0)
-    project(0)
-    gather_near(1)
+    gather_wait(0, 1)
+    swap = project(0)
+    gather_wait(1, 0)
+    gather_send(1, 1)
+    add_cores(0, swap)
     hand_out(0)
-    gather_far(1)
-    gather_relay(1)
     take_in(0)
-    gather_end(1)
-    project(1)
+    gather_wait(1, 1)
+    swap = project(1)
+    add_cores(1, swap)
     hand_out(1)
     take_in(1)
 
@@ -440,8 +438,10 @@
             pltpu.VMEM((ROWS + 1, ASK, KV), BF16),
             pltpu.VMEM((4, ASK, WIDE), BF16),
             pltpu.VMEM((4, ASK, WIDE), BF16),
-            pltpu.VMEM((2, 16, 16, 2048), BF16),
-            pltpu.VMEM((16, 16, 512), F32),
+            pltpu.VMEM((2, 16, 16, WIDTH[0]), BF16),
+            pltpu.VMEM((2, 16, 16, WIDTH[1]), BF16),
+            pltpu.VMEM((256, 768), BF16),
+            pltpu.VMEM((2, 16, 16, 512), F32),
             pltpu.VMEM((2, 8, 16, 512), BF16),
             pltpu.VMEM((2, 8, 16, 512), BF16),
             pltpu.VMEM((2, 8, 16, 512), BF16),
@@ -453,8 +453,8 @@
             sems((16,)),
             sems((7,)),
             sems((7,)),
-            sems((80,)),
-            sems((128,)),
+            sems((32,)),
+            sems((32,)),
             sems((16,)),
             sems((16,)),
         ],

time: 58.4 us -> 52.6 us (0.901)
  Pallas kernels: 56.7 us -> 50.9 us
    pallas_call x1, Pallas kernels: 56.7 us -> 50.9 us  [body(): pl.pallas_call(kernel, out_shape=jax.ShapeDtypeStruct((ROWS + 1, STEPS, 8...]
where the time goes in v3:
time: 52.6 us; the launch traced here: 52.4 us
  Pallas kernels  50.9 us (97%)
  local copies, waits for them, and re-layouts  1.49 us (3%)
    pallas_call x1, Pallas kernels, body(): pl.pallas_call(kernel, out_shape=jax.ShapeDtypeStruct((ROWS + 1, STEPS, 8...  50.9 us
    unnamed x1, local copies, waits for them, and re-layouts  1.49 us

profile of v3, /device:TPU:1, one launch (start us, length us, event | category | flops | bytes accessed | tf_op | source)
XLA Modules:
  0.0 52.4 jit_solution(10270258626572499809)
XLA Ops:
  0.0 50.9 %decode.1 = bf16[9,3,896]{2,1,0:T(4,128)(2,1)} custom-call(s32[1,8]{1,0:T(1,128)} %lengths.1, s32[1,16]{1,0:T(1,128)} %bitcast.19, bf16[9,3,3072]{2,1,0:T(4,128)(2,1)} %bitcast.17, bf16[9,3,576]{2,1,0:T(4,128)(2,1)} %bitcast.18, bf16[8,576,1536]{2,1,0:T(8,128)(2,1)} %bitcast.14, bf16[16,64,576]{2,1,0:T(8,128)(2,1)} %slices.1, bf16[16,128,512]{2,1,0:T(8,128)(2,1)} %w_key.1, ...), custom_call_target="tpu_custom_call" | custom-call | tf_op jit(solution)/shard_map/decode/pallas_call | solution.py:416
  50.9 1.5 %copy.11 = bf16[3,1,9,896]{3,0,2,1:T(4,128)(2,1)} copy(bf16[3,1,9,896]{3,0,2,1:T(4,128)(2,1)} %bitcast.16) | data formatting | bytes 96768

commit v4 on v3

--- a/solution.py
+++ b/solution.py
@@ -73,15 +73,10 @@
     load_wv = pltpu.make_async_copy(w_value, wv, dma.at[6])
     load_wo = pltpu.make_async_copy(w_out, wo.at[0:448], dma.at[7])
     load_qv.start()
-    load_sl.start()
     load_wk.start()
     load_lv.start()
     load_kt[0].start()
-    load_kt[1].start()
-    load_wv.start()
-    load_kt[2].start()
-    load_kt[3].start()
-    load_wo.start()
+    load_sl.start()
 
     barrier = pltpu.get_barrier_semaphore()
     for i in range(1, 16):
@@ -91,31 +86,6 @@
 
     qf[...] = jnp.zeros_like(qf)
     lat[...] = jnp.zeros_like(lat)
-    owners = [placement[0, i] for i in range(16)]
-    owner_of_lane = lax.broadcasted_iota(jnp.int32, (8, 16 * TOK), 1) // TOK
-    code = jnp.zeros((8, 16 * TOK), jnp.int32)
-    for i in range(16):
-        rank = jnp.int32(0)
-        for j in range(i):
-            rank = rank + jnp.where(owners[j] == owners[i], 1, 0)
-        code = jnp.where(owner_of_lane == i, owners[i] * CAP + rank, code)
-
-    wo[448:512, :] = jnp.zeros((64, 2048), BF16)
-    to_row = lax.broadcasted_iota(jnp.int32, (256, 256), 0)
-    from_row = lax.broadcasted_iota(jnp.int32, (256, 256), 1)
-    for b in range(3):
-        back = (to_row // 16 == from_row // 16) & (to_row % 16 == from_row % 16 - 12 + 4 * b) & (from_row % 16 >= 12)
-        unpack[:, 256 * b : 256 * b + 256] = jnp.where(back, 1.0, 0.0).astype(BF16)
-
-    slw[:, KV:WIDE] = jnp.ones((16 * TOK, WIDE - KV), BF16)
-    at0 = lax.broadcasted_iota(jnp.int32, (16 * TOK, 16 * TOK), 0)
-    at1 = lax.broadcasted_iota(jnp.int32, (16 * TOK, 16 * TOK), 1)
-    chosen = (at0 % TOK == at1 % TOK) & ((at0 // TOK) * CAP + c == code[0:1, :])
-    selector = jnp.where(chosen, 1.0, 0.0).astype(BF16)
-    load_sl.wait()
-    slw[:, 0 : KV + ROPE] = sl[...].reshape(16 * TOK, KV + ROPE)
-    k_send[...] = nn(selector, slw[...]).astype(BF16).reshape(16, TOK, WIDE)
-
     load_qv.wait()
     load_lv.wait()
     for r in range(ROWS + 1):
@@ -124,17 +94,9 @@
         qf[r, PAD : PAD + STEPS, :] = v
         lat[r, 0:STEPS, :] = lv[r].astype(F32)
 
-    pl.semaphore_wait(barrier, 22)
-
-    slice_sends = []
-    for i in range(1, 16):
-        to = (g + i) % 16
-        cp = remote(k_send.at[to], k8.at[c, pl.ds(TOK * g, TOK)], sl_s.at[i], sl_r.at[i], (to, h))
-        cp.start()
-        slice_sends.append(cp)
-    k8[c, pl.ds(TOK * g, TOK), :] = k_send[g]
-
     load_wk.wait()
+    load_kt[1].start()
+    load_wv.start()
     row = lax.broadcasted_iota(jnp.int32, (72, 128), 0)
     lane = lax.broadcasted_iota(jnp.int32, (72, 128), 1)
     first = row % 8 < PAD
@@ -152,6 +114,8 @@
             parts.append(jnp.concatenate([absorbed, rope], axis=1).reshape(9, 8, WIDE))
         q_all[:, 16 * quad : 16 * quad + 16, :] = jnp.concatenate(parts, axis=1).astype(BF16)
 
+    pl.semaphore_wait(barrier, 22)
+
     ask_sib = remote(q_all.at[pl.ds(4 * (1 - c), 4)], q_sib, sib_s.at[0], sib_r.at[0], sib)
     ask_sib.start()
     ask_z = []
@@ -161,12 +125,51 @@
         cp.start()
         ask_z.append(cp)
     q8[z] = q_all[8]
+
+    owners = [placement[0, i] for i in range(16)]
+    owner_of_lane = lax.broadcasted_iota(jnp.int32, (8, 16 * TOK), 1) // TOK
+    code = jnp.zeros((8, 16 * TOK), jnp.int32)
+    for i in range(16):
+        rank = jnp.int32(0)
+        for j in range(i):
+            rank = rank + jnp.where(owners[j] == owners[i], 1, 0)
+        code = jnp.where(owner_of_lane == i, owners[i] * CAP + rank, code)
+
+    wo[448:512, :] = jnp.zeros((64, 2048), BF16)
+    to_row = lax.broadcasted_iota(jnp.int32, (256, 256), 0)
+    from_row = lax.broadcasted_iota(jnp.int32, (256, 256), 1)
+    for b in range(3):
+        back = (to_row // 16 == from_row // 16) & (to_row % 16 == from_row % 16 - 12 + 4 * b) & (from_row % 16 >= 12)
+        unpack[:, 256 * b : 256 * b + 256] = jnp.where(back, 1.0, 0.0).astype(BF16)
+
+    slw[:, KV:WIDE] = jnp.ones((16 * TOK, WIDE - KV), BF16)
+    at0 = lax.broadcasted_iota(jnp.int32, (16 * TOK, 16 * TOK), 0)
+    at1 = lax.broadcasted_iota(jnp.int32, (16 * TOK, 16 * TOK), 1)
+    chosen = (at0 % TOK == at1 % TOK) & ((at0 // TOK) * CAP + c == code[0:1, :])
+    selector = jnp.where(chosen, 1.0, 0.0).astype(BF16)
+    load_sl.wait()
+    slw[:, 0 : KV + ROPE] = sl[...].reshape(16 * TOK, KV + ROPE)
+    k_send[...] = nn(selector, slw[...]).astype(BF16).reshape(16, TOK, WIDE)
+
+    slice_sends = []
+    for i in range(1, 16):
+        to = (g + i) % 16
+        cp = remote(k_send.at[to], k8.at[c, pl.ds(TOK * g, TOK)], sl_s.at[i], sl_r.at[i], (to, h))
+        cp.start()
+        slice_sends.append(cp)
+    k8[c, pl.ds(TOK * g, TOK), :] = k_send[g]
+
     ask_sib.wait()
 
     recent_ok = step_mask(2 * ASK, 16)
 
     def resident(i):
         load_kt[i].wait()
+        if i == 0:
+            load_kt[2].start()
+        if i == 1:
+            load_kt[3].start()
+            load_wo.start()
         q = jnp.concatenate([q_all[4 * c + i], q_sib[i]], axis=0)[:, 0 : KV + ROPE]
         recent = lat[4 * c + i].astype(BF16)
         s = nn(q, kt[i])
@@ -308,9 +311,7 @@
         lane = lax.broadcasted_iota(jnp.int32, (16, 128), 1)
         middle = jnp.where(lane < 64, sums[0][:, 384:512], shifted[:, 0:128])
         mixed = jnp.concatenate([sums[0][:, 0:384], middle, shifted[:, 128:512]], axis=1)
-        rows = (0, 1, 4, 5) if part == 0 else (2, 3, 6, 7, 8)
-        for a, r in enumerate(rows):
-            out[r] = mixed[STEPS * a : STEPS * a + STEPS].astype(BF16)
+        return mixed.astype(BF16)
 
     lat_sends = [resident(0), resident(1)]
     for cp in lat_sends:
@@ -386,20 +387,27 @@
         cp.wait()
     values(1)
     gather_send(1, 0)
+    gather_wait(1, 0)
+    gather_send(1, 1)
 
     load_wo.wait()
     gather_wait(0, 1)
     swap = project(0)
-    gather_wait(1, 0)
-    gather_send(1, 1)
     add_cores(0, swap)
     hand_out(0)
-    take_in(0)
     gather_wait(1, 1)
     swap = project(1)
+    sums_a = take_in(0)
     add_cores(1, swap)
     hand_out(1)
-    take_in(1)
+    sums_b = take_in(1)
+
+    to_row = lax.broadcasted_iota(jnp.int32, (32, 32), 0)
+    from_row = lax.broadcasted_iota(jnp.int32, (32, 32), 1)
+    r = to_row // STEPS
+    source = jnp.where(r >= ROWS, 16 + 4 * STEPS, r // 2 % 2 * 16 + (r // 4 * 2 + r % 2) * STEPS) + to_row % STEPS
+    order = jnp.where(source == from_row, 1.0, 0.0).astype(BF16)
+    out[...] = nn(order, jnp.concatenate([sums_a, sums_b], axis=0)).astype(BF16)
 
     for part in (0, 1):
         for i in range(8):
@@ -415,7 +423,7 @@
     sems = pltpu.SemaphoreType.DMA
     out = pl.pallas_call(
         kernel,
-        out_shape=jax.ShapeDtypeStruct((ROWS + 1, STEPS, 896), BF16),
+        out_shape=jax.ShapeDtypeStruct((32, 896), BF16),
         in_specs=[smem, smem] + [anywhere] * 7,
         out_specs=vmem,
         scratch_shapes=[
@@ -473,7 +481,8 @@
         w_value,
         jnp.swapaxes(w_out, 0, 1),
     )
-    return jnp.swapaxes(out, 0, 1)[:, None]
+    mixed = out[: STEPS * (ROWS + 1)].reshape(ROWS + 1, STEPS, 896)
+    return jnp.swapaxes(mixed, 0, 1)[:, None]
 
 
 def solution(mesh):

time: 52.6 us -> 49.9 us (0.949)
  Pallas kernels: 50.9 us -> 48.2 us
    pallas_call x1, Pallas kernels: 50.9 us -> 48.2 us  [body(): pl.pallas_call(kernel, out_shape=jax.ShapeDtypeStruct((32, 896), BF16), i...]
    reshape x0 -> x1, local copies, waits for them, and re-layouts: none -> 1.49 us  [body(): mixed = out[:STEPS * (ROWS + 1)].reshape(ROWS + 1, STEPS, 896)]
    unnamed x1 -> x0, local copies, waits for them, and re-layouts: 1.49 us -> none
where the time goes in v4:
time: 49.9 us; the launch traced here: 49.7 us
  Pallas kernels  48.2 us (97%)
  local copies, waits for them, and re-layouts  1.49 us (3%)
    pallas_call x1, Pallas kernels, body(): pl.pallas_call(kernel, out_shape=jax.ShapeDtypeStruct((32, 896), BF16), i...  48.2 us
    reshape x1, local copies, waits for them, and re-layouts, body(): mixed = out[:STEPS * (ROWS + 1)].reshape(ROWS + 1, STEPS, 896)  1.49 us

profile of v4, /device:TPU:1, one launch (start us, length us, event | category | flops | bytes accessed | tf_op | source)
XLA Modules:
  0.0 49.7 jit_solution(3101862463173493712)
XLA Ops:
  0.0 48.2 %decode.1 = bf16[32,896]{1,0:T(8,128)(2,1)} custom-call(s32[1,8]{1,0:T(1,128)} %lengths.1, s32[1,16]{1,0:T(1,128)} %bitcast.20, bf16[9,3,3072]{2,1,0:T(4,128)(2,1)} %bitcast.18, bf16[9,3,576]{2,1,0:T(4,128)(2,1)} %bitcast.19, bf16[8,576,1536]{2,1,0:T(8,128)(2,1)} %bitcast.15, bf16[16,64,576]{2,1,0:T(8,128)(2,1)} %slices.1, bf16[16,128,512]{2,1,0:T(8,128)(2,1)} %w_key.1, ...), custom_call_target="tpu_custom_call" | custom-call | tf_op jit(solution)/shard_map/decode/pallas_call | solution.py:424
  48.3 1.5 %reshape.7 = bf16[9,3,896]{2,1,0:T(4,128)(2,1)} reshape(bf16[27,896]{1,0:T(8,128)(2,1)} %bitcast.17) | data formatting | bytes 96768 | tf_op jit(solution)/shard_map/reshape | solution.py:484

commit v5 on v4

--- a/solution.py
+++ b/solution.py
@@ -72,17 +72,45 @@
     load_kt = [pltpu.make_async_copy(cache.at[4 * c + i], kt.at[i], dma.at[2 + i]) for i in range(4)]
     load_wv = pltpu.make_async_copy(w_value, wv, dma.at[6])
     load_wo = pltpu.make_async_copy(w_out, wo.at[0:448], dma.at[7])
+    load_sl.start()
     load_qv.start()
+    load_lv.start()
     load_wk.start()
-    load_lv.start()
     load_kt[0].start()
-    load_sl.start()
 
     barrier = pltpu.get_barrier_semaphore()
     for i in range(1, 16):
         pl.semaphore_signal(barrier, inc=1, device_id=((g + i) % 16, h), device_id_type=MESH)
     for i in range(1, 8):
         pl.semaphore_signal(barrier, inc=1, device_id=(g, (h + i) % 8), device_id_type=MESH)
+
+    owners = [placement[0, i] for i in range(16)]
+    owner_of_lane = lax.broadcasted_iota(jnp.int32, (8, 16 * TOK), 1) // TOK
+    code = jnp.zeros((8, 16 * TOK), jnp.int32)
+    for i in range(16):
+        rank = jnp.int32(0)
+        for j in range(i):
+            rank = rank + jnp.where(owners[j] == owners[i], 1, 0)
+        code = jnp.where(owner_of_lane == i, owners[i] * CAP + rank, code)
+
+    slw[:, KV:WIDE] = jnp.ones((16 * TOK, WIDE - KV), BF16)
+    at0 = lax.broadcasted_iota(jnp.int32, (16 * TOK, 16 * TOK), 0)
+    at1 = lax.broadcasted_iota(jnp.int32, (16 * TOK, 16 * TOK), 1)
+    chosen = (at0 % TOK == at1 % TOK) & ((at0 // TOK) * CAP + c == code[0:1, :])
+    selector = jnp.where(chosen, 1.0, 0.0).astype(BF16)
+    load_sl.wait()
+    slw[:, 0 : KV + ROPE] = sl[...].reshape(16 * TOK, KV + ROPE)
+    k_send[...] = nn(selector, slw[...]).astype(BF16).reshape(16, TOK, WIDE)
+
+    pl.semaphore_wait(barrier, 22)
+
+    slice_sends = []
+    for i in range(1, 16):
+        to = (g + i) % 16
+        cp = remote(k_send.at[to], k8.at[c, pl.ds(TOK * g, TOK)], sl_s.at[i], sl_r.at[i], (to, h))
+        cp.start()
+        slice_sends.append(cp)
+    k8[c, pl.ds(TOK * g, TOK), :] = k_send[g]
 
     qf[...] = jnp.zeros_like(qf)
     lat[...] = jnp.zeros_like(lat)
@@ -114,8 +142,6 @@
             parts.append(jnp.concatenate([absorbed, rope], axis=1).reshape(9, 8, WIDE))
         q_all[:, 16 * quad : 16 * quad + 16, :] = jnp.concatenate(parts, axis=1).astype(BF16)
 
-    pl.semaphore_wait(barrier, 22)
-
     ask_sib = remote(q_all.at[pl.ds(4 * (1 - c), 4)], q_sib, sib_s.at[0], sib_r.at[0], sib)
     ask_sib.start()
     ask_z = []
@@ -126,38 +152,12 @@
         ask_z.append(cp)
     q8[z] = q_all[8]
 
-    owners = [placement[0, i] for i in range(16)]
-    owner_of_lane = lax.broadcasted_iota(jnp.int32, (8, 16 * TOK), 1) // TOK
-    code = jnp.zeros((8, 16 * TOK), jnp.int32)
-    for i in range(16):
-        rank = jnp.int32(0)
-        for j in range(i):
-            rank = rank + jnp.where(owners[j] == owners[i], 1, 0)
-        code = jnp.where(owner_of_lane == i, owners[i] * CAP + rank, code)
-
     wo[448:512, :] = jnp.zeros((64, 2048), BF16)
     to_row = lax.broadcasted_iota(jnp.int32, (256, 256), 0)
     from_row = lax.broadcasted_iota(jnp.int32, (256, 256), 1)
     for b in range(3):
         back = (to_row // 16 == from_row // 16) & (to_row % 16 == from_row % 16 - 12 + 4 * b) & (from_row % 16 >= 12)
         unpack[:, 256 * b : 256 * b + 256] = jnp.where(back, 1.0, 0.0).astype(BF16)
-
-    slw[:, KV:WIDE] = jnp.ones((16 * TOK, WIDE - KV), BF16)
-    at0 = lax.broadcasted_iota(jnp.int32, (16 * TOK, 16 * TOK), 0)
-    at1 = lax.broadcasted_iota(jnp.int32, (16 * TOK, 16 * TOK), 1)
-    chosen = (at0 % TOK == at1 % TOK) & ((at0 // TOK) * CAP + c == code[0:1, :])
-    selector = jnp.where(chosen, 1.0, 0.0).astype(BF16)
-    load_sl.wait()
-    slw[:, 0 : KV + ROPE] = sl[...].reshape(16 * TOK, KV + ROPE)
-    k_send[...] = nn(selector, slw[...]).astype(BF16).reshape(16, TOK, WIDE)
-
-    slice_sends = []
-    for i in range(1, 16):
-        to = (g + i) % 16
-        cp = remote(k_send.at[to], k8.at[c, pl.ds(TOK * g, TOK)], sl_s.at[i], sl_r.at[i], (to, h))
-        cp.start()
-        slice_sends.append(cp)
-    k8[c, pl.ds(TOK * g, TOK), :] = k_send[g]
 
     ask_sib.wait()
 
@@ -250,6 +250,34 @@
                 ref = blocks_of(part, k, ring, d)
                 remote(ref, ref, ag_s.at[n], ag_r.at[n], along(ring if k == 0 else 1 - ring, d)).wait_recv()
 
+    def one_block(part, k, d1, d2):
+        one, two = (x, y) if k == 0 else (y, x)
+        return gath[part].at[k, pl.ds(4 * ((two - d2) % 4) + (one - d1) % 4, 1)]
+
+    def pass_on(part, k, d1):
+        ref = one_block(part, k, d1, 0)
+        for d in (2, 1, 3):
+            n = 32 + (k * 4 + d1) * 4 + d
+            cp = remote(ref, ref, ag_s.at[n], ag_r.at[n], along(1 - k, d))
+            cp.start()
+            ag_sends.append(cp)
+
+    def gather_blocks(part):
+        for d in (1, 3, 2):
+            for k in (0, 1):
+                n = ((part * 2 + k) * 2) * 4 + d
+                ref = blocks_of(part, k, 0, d)
+                remote(ref, ref, ag_s.at[n], ag_r.at[n], along(k, d)).wait_recv()
+                pass_on(part, k, d)
+
+    def gather_last(part):
+        for k in (0, 1):
+            for d1 in (0, 1, 3, 2):
+                for d2 in (1, 3, 2):
+                    n = 32 + (k * 4 + d1) * 4 + d2
+                    ref = one_block(part, k, d1, d2)
+                    remote(ref, ref, ag_s.at[n], ag_r.at[n], along(1 - k, d2)).wait_recv()
+
     def project(part):
         half = WIDTH[part]
         first_half = gath[part][0].reshape(256, half)
@@ -314,19 +342,16 @@
         return mixed.astype(BF16)
 
     lat_sends = [resident(0), resident(1)]
+
+    for cp in slice_sends:
+        cp.wait()
+    keys_sib = remote(k8.at[c], k8.at[c], sib_s.at[5], sib_r.at[5], sib)
+    keys_sib.start()
     for cp in lat_sends:
         cp.wait()
     load_wv.wait()
     values(0)
     gather_send(0, 0)
-
-    for cp in slice_sends:
-        cp.wait()
-    keys_sib = remote(k8.at[c], k8.at[c], sib_s.at[5], sib_r.at[5], sib)
-    keys_sib.start()
-    lat_sends = [resident(2)]
-    gather_wait(0, 0)
-    gather_send(0, 1)
 
     for cp in ask_z:
         cp.wait()
@@ -356,6 +381,9 @@
         part_z.append(cp)
     o8[z] = o8_send[z]
 
+    lat_sends = [resident(2)]
+    gather_wait(0, 0)
+    gather_send(0, 1)
     lat_sends.append(resident(3))
 
     q = q_all[8][:, 0 : KV + ROPE]
@@ -387,15 +415,16 @@
         cp.wait()
     values(1)
     gather_send(1, 0)
-    gather_wait(1, 0)
-    gather_send(1, 1)
+    for k in (0, 1):
+        pass_on(1, k, 0)
+    gather_blocks(1)
 
     load_wo.wait()
     gather_wait(0, 1)
     swap = project(0)
     add_cores(0, swap)
     hand_out(0)
-    gather_wait(1, 1)
+    gather_last(1)
     swap = project(1)
     sums_a = take_in(0)
     add_cores(1, swap)
@@ -461,8 +490,8 @@
             sems((16,)),
             sems((7,)),
             sems((7,)),
-            sems((32,)),
-            sems((32,)),
+            sems((64,)),
+            sems((64,)),
             sems((16,)),
             sems((16,)),
         ],

time: 49.9 us -> 48.5 us (0.972)
  Pallas kernels: 48.2 us -> 46.9 us
    pallas_call x1, Pallas kernels: 48.2 us -> 46.9 us  [body(): pl.pallas_call(kernel, out_shape=jax.ShapeDtypeStruct((32, 896), BF16), i...]
where the time goes in v5:
time: 48.5 us; the launch traced here: 48.4 us
  Pallas kernels  46.9 us (97%)
  local copies, waits for them, and re-layouts  1.49 us (3%)
    pallas_call x1, Pallas kernels, body(): pl.pallas_call(kernel, out_shape=jax.ShapeDtypeStruct((32, 896), BF16), i...  46.9 us
    reshape x1, local copies, waits for them, and re-layouts, body(): mixed = out[:STEPS * (ROWS + 1)].reshape(ROWS + 1, STEPS, 896)  1.49 us

profile of v5, /device:TPU:1, one launch (start us, length us, event | category | flops | bytes accessed | tf_op | source)
XLA Modules:
  0.0 48.4 jit_solution(6024767656964434209)
XLA Ops:
  0.0 46.9 %decode.1 = bf16[32,896]{1,0:T(8,128)(2,1)} custom-call(s32[1,8]{1,0:T(1,128)} %lengths.1, s32[1,16]{1,0:T(1,128)} %bitcast.20, bf16[9,3,3072]{2,1,0:T(4,128)(2,1)} %bitcast.18, bf16[9,3,576]{2,1,0:T(4,128)(2,1)} %bitcast.19, bf16[8,576,1536]{2,1,0:T(8,128)(2,1)} %bitcast.15, bf16[16,64,576]{2,1,0:T(8,128)(2,1)} %slices.1, bf16[16,128,512]{2,1,0:T(8,128)(2,1)} %w_key.1, ...), custom_call_target="tpu_custom_call" | custom-call | tf_op jit(solution)/shard_map/decode/pallas_call | solution.py:453
  46.9 1.5 %reshape.7 = bf16[9,3,896]{2,1,0:T(4,128)(2,1)} reshape(bf16[27,896]{1,0:T(8,128)(2,1)} %bitcast.17) | data formatting | bytes 96768 | tf_op jit(solution)/shard_map/reshape | solution.py:513

commit v6 on v5

--- a/solution.py
+++ b/solution.py
@@ -27,6 +27,7 @@
 HEADS = 16
 ASK = HEADS * PAD
 WIDTH = (768, 1024)
+TIGHT = HEADS * STEPS
 TOK = 16
 
 
@@ -44,8 +45,8 @@
     return jnp.dot(a, b, preferred_element_type=F32)
 
 
-def step_mask(rows, width):
-    step = lax.broadcasted_iota(jnp.int32, (rows, width), 0) % PAD
+def step_mask(rows, width, steps=PAD):
+    step = lax.broadcasted_iota(jnp.int32, (rows, width), 0) % steps
     at = lax.broadcasted_iota(jnp.int32, (rows, width), 1)
     return (at < STEPS) & (at <= step)
 
@@ -54,7 +55,7 @@
     lengths, placement, queries, latents, cache, slices, w_key, w_value, w_out,
     out,
     kt, wk, wv, wo, sl, slw, k_send, qv, lv, qf, lat,
-    q_all, q_sib, q8, k8, o_sib, lt, o8_send, o8,
+    q_all, q_sib, q8_mine, q8, k8, o_sib, lt, o8_send, o8,
     gath_a, gath_b, unpack, p_all, p_send, p_recv, p_sum, red,
     dma, sib_s, sib_r, sl_s, sl_r, z_s, z_r, ag_s, ag_r, red_s, red_r,
 ):
@@ -72,10 +73,10 @@
     load_kt = [pltpu.make_async_copy(cache.at[4 * c + i], kt.at[i], dma.at[2 + i]) for i in range(4)]
     load_wv = pltpu.make_async_copy(w_value, wv, dma.at[6])
     load_wo = pltpu.make_async_copy(w_out, wo.at[0:448], dma.at[7])
-    load_sl.start()
     load_qv.start()
     load_lv.start()
     load_wk.start()
+    load_sl.start()
     load_kt[0].start()
 
     barrier = pltpu.get_barrier_semaphore()
@@ -83,34 +84,6 @@
         pl.semaphore_signal(barrier, inc=1, device_id=((g + i) % 16, h), device_id_type=MESH)
     for i in range(1, 8):
         pl.semaphore_signal(barrier, inc=1, device_id=(g, (h + i) % 8), device_id_type=MESH)
-
-    owners = [placement[0, i] for i in range(16)]
-    owner_of_lane = lax.broadcasted_iota(jnp.int32, (8, 16 * TOK), 1) // TOK
-    code = jnp.zeros((8, 16 * TOK), jnp.int32)
-    for i in range(16):
-        rank = jnp.int32(0)
-        for j in range(i):
-            rank = rank + jnp.where(owners[j] == owners[i], 1, 0)
-        code = jnp.where(owner_of_lane == i, owners[i] * CAP + rank, code)
-
-    slw[:, KV:WIDE] = jnp.ones((16 * TOK, WIDE - KV), BF16)
-    at0 = lax.broadcasted_iota(jnp.int32, (16 * TOK, 16 * TOK), 0)
-    at1 = lax.broadcasted_iota(jnp.int32, (16 * TOK, 16 * TOK), 1)
-    chosen = (at0 % TOK == at1 % TOK) & ((at0 // TOK) * CAP + c == code[0:1, :])
-    selector = jnp.where(chosen, 1.0, 0.0).astype(BF16)
-    load_sl.wait()
-    slw[:, 0 : KV + ROPE] = sl[...].reshape(16 * TOK, KV + ROPE)
-    k_send[...] = nn(selector, slw[...]).astype(BF16).reshape(16, TOK, WIDE)
-
-    pl.semaphore_wait(barrier, 22)
-
-    slice_sends = []
-    for i in range(1, 16):
-        to = (g + i) % 16
-        cp = remote(k_send.at[to], k8.at[c, pl.ds(TOK * g, TOK)], sl_s.at[i], sl_r.at[i], (to, h))
-        cp.start()
-        slice_sends.append(cp)
-    k8[c, pl.ds(TOK * g, TOK), :] = k_send[g]
 
     qf[...] = jnp.zeros_like(qf)
     lat[...] = jnp.zeros_like(lat)
@@ -142,15 +115,23 @@
             parts.append(jnp.concatenate([absorbed, rope], axis=1).reshape(9, 8, WIDE))
         q_all[:, 16 * quad : 16 * quad + 16, :] = jnp.concatenate(parts, axis=1).astype(BF16)
 
-    ask_sib = remote(q_all.at[pl.ds(4 * (1 - c), 4)], q_sib, sib_s.at[0], sib_r.at[0], sib)
-    ask_sib.start()
-    ask_z = []
-    for i in range(1, 4):
-        to = (z + i) % 4
-        cp = remote(q_all.at[8], q8.at[z], z_s.at[i], z_r.at[i], (g, 2 * to + c))
-        cp.start()
-        ask_z.append(cp)
-    q8[z] = q_all[8]
+    owners = [placement[0, i] for i in range(16)]
+    owner_of_lane = lax.broadcasted_iota(jnp.int32, (8, 16 * TOK), 1) // TOK
+    code = jnp.zeros((8, 16 * TOK), jnp.int32)
+    for i in range(16):
+        rank = jnp.int32(0)
+        for j in range(i):
+            rank = rank + jnp.where(owners[j] == owners[i], 1, 0)
+        code = jnp.where(owner_of_lane == i, owners[i] * CAP + rank, code)
+
+    slw[:, KV:WIDE] = jnp.ones((16 * TOK, WIDE - KV), BF16)
+    at0 = lax.broadcasted_iota(jnp.int32, (16 * TOK, 16 * TOK), 0)
+    at1 = lax.broadcasted_iota(jnp.int32, (16 * TOK, 16 * TOK), 1)
+    chosen = (at0 % TOK == at1 % TOK) & ((at0 // TOK) * CAP + c == code[0:1, :])
+    selector = jnp.where(chosen, 1.0, 0.0).astype(BF16)
+    load_sl.wait()
+    slw[:, 0 : KV + ROPE] = sl[...].reshape(16 * TOK, KV + ROPE)
+    k_send[...] = nn(selector, slw[...]).astype(BF16).reshape(16, TOK, WIDE)
 
     wo[448:512, :] = jnp.zeros((64, 2048), BF16)
     to_row = lax.broadcasted_iota(jnp.int32, (256, 256), 0)
@@ -158,6 +139,30 @@
     for b in range(3):
         back = (to_row // 16 == from_row // 16) & (to_row % 16 == from_row % 16 - 12 + 4 * b) & (from_row % 16 >= 12)
         unpack[:, 256 * b : 256 * b + 256] = jnp.where(back, 1.0, 0.0).astype(BF16)
+
+    tight = (lax.broadcasted_iota(jnp.int32, (TIGHT, ASK), 0), lax.broadcasted_iota(jnp.int32, (TIGHT, ASK), 1))
+    tight = jnp.where((tight[0] // STEPS == tight[1] // PAD) & (tight[0] % STEPS == tight[1] % PAD), 1.0, 0.0)
+    q8_mine[...] = nn(tight.astype(BF16), q_all[8]).astype(BF16)
+
+    pl.semaphore_wait(barrier, 22)
+
+    ask_sib = remote(q_all.at[pl.ds(4 * (1 - c), 4)], q_sib, sib_s.at[0], sib_r.at[0], sib)
+    ask_sib.start()
+    ask_z = []
+    for i in range(1, 4):
+        to = (z + i) % 4
+        cp = remote(q8_mine, q8.at[z], z_s.at[i], z_r.at[i], (g, 2 * to + c))
+        cp.start()
+        ask_z.append(cp)
+    q8[z] = q8_mine[...]
+
+    slice_sends = []
+    for i in range(1, 16):
+        to = (g + i) % 16
+        cp = remote(k_send.at[to], k8.at[c, pl.ds(TOK * g, TOK)], sl_s.at[i], sl_r.at[i], (to, h))
+        cp.start()
+        slice_sends.append(cp)
+    k8[c, pl.ds(TOK * g, TOK), :] = k_send[g]
 
     ask_sib.wait()
 
@@ -357,7 +362,7 @@
         cp.wait()
     keys_sib.wait()
     keys = k8[...].reshape(2 * 16 * TOK, WIDE)
-    q = q8[...].reshape(4 * ASK, WIDE)
+    q = q8[...].reshape(4 * TIGHT, WIDE)
     flag = (lax.broadcasted_iota(jnp.int32, (8, WIDE), 1) == KV + ROPE).astype(BF16)
     present = nt(flag, keys)[0:1] > 0.5
     s = jnp.where(present, nt(q, keys), LOWEST)
@@ -365,14 +370,14 @@
     e = jnp.exp((s - m) * SCALE)
     total = jnp.sum(e, axis=1, keepdims=True)
     o = nn(e.astype(BF16), keys[:, 0:KV])
-    lane = lax.broadcasted_iota(jnp.int32, (4 * ASK, 128), 1)
-    stats = jnp.zeros((4 * ASK, 128), F32)
+    lane = lax.broadcasted_iota(jnp.int32, (4 * TIGHT, 128), 1)
+    stats = jnp.zeros((4 * TIGHT, 128), F32)
     for n, rest in enumerate((m, total)):
         for t in range(3):
             piece = rest.astype(BF16).astype(F32)
             rest = rest - piece
             stats = jnp.where(lane == 3 * n + t, piece, stats)
-    o8_send[...] = jnp.concatenate([o, stats], axis=1).astype(BF16).reshape(4, ASK, WIDE)
+    o8_send[...] = jnp.concatenate([o, stats], axis=1).astype(BF16).reshape(4, TIGHT, WIDE)
     part_z = []
     for i in range(1, 4):
         to = (z + i) % 4
@@ -386,9 +391,9 @@
     gather_send(0, 1)
     lat_sends.append(resident(3))
 
-    q = q_all[8][:, 0 : KV + ROPE]
+    q = q8_mine[:, 0 : KV + ROPE]
     recent = lat[8].astype(BF16)
-    s_new = jnp.where(step_mask(ASK, 16), nt(q, recent), LOWEST)
+    s_new = jnp.where(step_mask(TIGHT, 16, STEPS), nt(q, recent), LOWEST)
     m_new = jnp.max(s_new, axis=1, keepdims=True)
     e_new = jnp.exp((s_new - m_new) * SCALE)
     total_new = jnp.sum(e_new, axis=1, keepdims=True)
@@ -410,7 +415,9 @@
         weight = jnp.exp((m_part[i] - m) * SCALE)
         o = o + o8[i][:, 0:KV].astype(F32) * weight
         total = total + total_part[i] * weight
-    lt[8] = (o / total).astype(BF16)
+    loose = (lax.broadcasted_iota(jnp.int32, (ASK, TIGHT), 0), lax.broadcasted_iota(jnp.int32, (ASK, TIGHT), 1))
+    loose = jnp.where((loose[0] // PAD == loose[1] // STEPS) & (loose[0] % PAD == loose[1] % STEPS), 1.0, 0.0)
+    lt[8] = nn(loose.astype(BF16), (o / total).astype(BF16)).astype(BF16)
     for cp in lat_sends:
         cp.wait()
     values(1)
@@ -431,12 +438,14 @@
     hand_out(1)
     sums_b = take_in(1)
 
-    to_row = lax.broadcasted_iota(jnp.int32, (32, 32), 0)
-    from_row = lax.broadcasted_iota(jnp.int32, (32, 32), 1)
-    r = to_row // STEPS
-    source = jnp.where(r >= ROWS, 16 + 4 * STEPS, r // 2 % 2 * 16 + (r // 4 * 2 + r % 2) * STEPS) + to_row % STEPS
+    to_row = lax.broadcasted_iota(jnp.int32, (16 * STEPS, 32), 0)
+    from_row = lax.broadcasted_iota(jnp.int32, (16 * STEPS, 32), 1)
+    r = to_row % 16
+    source = jnp.where(r >= ROWS, 16 + 4 * STEPS, r // 2 % 2 * 16 + (r // 4 * 2 + r % 2) * STEPS) + to_row // 16
     order = jnp.where(source == from_row, 1.0, 0.0).astype(BF16)
-    out[...] = nn(order, jnp.concatenate([sums_a, sums_b], axis=0)).astype(BF16)
+    mixed = nn(order, jnp.concatenate([sums_a, sums_b], axis=0)).astype(BF16)
+    for t in range(STEPS):
+        out[t] = mixed[16 * t : 16 * t + ROWS + 1]
 
     for part in (0, 1):
         for i in range(8):
@@ -452,7 +461,7 @@
     sems = pltpu.SemaphoreType.DMA
     out = pl.pallas_call(
         kernel,
-        out_shape=jax.ShapeDtypeStruct((32, 896), BF16),
+        out_shape=jax.ShapeDtypeStruct((STEPS, ROWS + 1, 896), BF16),
         in_specs=[smem, smem] + [anywhere] * 7,
         out_specs=vmem,
         scratch_shapes=[
@@ -469,12 +478,13 @@
             pltpu.VMEM((ROWS + 1, 16, KV + ROPE), F32),
             pltpu.VMEM((ROWS + 1, ASK, WIDE), BF16),
             pltpu.VMEM((4, ASK, WIDE), BF16),
-            pltpu.VMEM((4, ASK, WIDE), BF16),
+            pltpu.VMEM((TIGHT, WIDE), BF16),
+            pltpu.VMEM((4, TIGHT, WIDE), BF16),
             pltpu.VMEM((2, 16 * TOK, WIDE), BF16),
             pltpu.VMEM((4, ASK, KV), BF16),
             pltpu.VMEM((ROWS + 1, ASK, KV), BF16),
-            pltpu.VMEM((4, ASK, WIDE), BF16),
-            pltpu.VMEM((4, ASK, WIDE), BF16),
+            pltpu.VMEM((4, TIGHT, WIDE), BF16),
+            pltpu.VMEM((4, TIGHT, WIDE), BF16),
             pltpu.VMEM((2, 16, 16, WIDTH[0]), BF16),
             pltpu.VMEM((2, 16, 16, WIDTH[1]), BF16),
             pltpu.VMEM((256, 768), BF16),
@@ -510,8 +520,7 @@
         w_value,
         jnp.swapaxes(w_out, 0, 1),
     )
-    mixed = out[: STEPS * (ROWS + 1)].reshape(ROWS + 1, STEPS, 896)
-    return jnp.swapaxes(mixed, 0, 1)[:, None]
+    return out[:, None]
 
 
 def solution(mesh):

time: 48.5 us -> 47.8 us (0.986)
  Pallas kernels: 46.9 us -> 46.1 us
    broadcast_in_dim x0 -> x1, local copies, waits for them, and re-layouts: none -> 1.54 us  [body(): return out[:, None]]
    reshape x1 -> x0, local copies, waits for them, and re-layouts: 1.49 us -> none  [body(): mixed = out[:STEPS * (ROWS + 1)].reshape(ROWS + 1, STEPS, 896)]
    pallas_call x1, Pallas kernels: 46.9 us -> 46.1 us  [body(): pl.pallas_call(kernel, out_shape=jax.ShapeDtypeStruct((STEPS, ROWS + 1, 8...]
where the time goes in v6:
time: 47.8 us; the launch traced here: 47.7 us
  Pallas kernels  46.1 us (96%)
  local copies, waits for them, and re-layouts  1.54 us (3%)
    pallas_call x1, Pallas kernels, body(): pl.pallas_call(kernel, out_shape=jax.ShapeDtypeStruct((STEPS, ROWS + 1, 8...  46.1 us
    broadcast_in_dim x1, local copies, waits for them, and re-layouts, body(): return out[:, None]  1.54 us

profile of v6, /device:TPU:1, one launch (start us, length us, event | category | flops | bytes accessed | tf_op | source)
XLA Modules:
  0.0 47.7 jit_solution(17082282015596903177)
XLA Ops:
  0.0 46.1 %decode.1 = bf16[3,9,896]{2,1,0:T(8,128)(2,1)} custom-call(s32[1,8]{1,0:T(1,128)} %lengths.1, s32[1,16]{1,0:T(1,128)} %bitcast.17, bf16[9,3,3072]{2,1,0:T(4,128)(2,1)} %bitcast.15, bf16[9,3,576]{2,1,0:T(4,128)(2,1)} %bitcast.16, bf16[8,576,1536]{2,1,0:T(8,128)(2,1)} %bitcast.12, bf16[16,64,576]{2,1,0:T(8,128)(2,1)} %slices.1, bf16[16,128,512]{2,1,0:T(8,128)(2,1)} %w_key.1, ...), custom_call_target="tpu_custom_call" | custom-call | tf_op jit(solution)/shard_map/decode/pallas_call | solution.py:462
  46.1 1.5 %copy.10 = bf16[3,1,9,896]{3,0,2,1:T(4,128)(2,1)} copy(bf16[3,1,9,896]{3,2,0,1:T(8,128)(2,1)} %bitcast.14) | data formatting | bytes 96768 | tf_op jit(solution)/shard_map/broadcast_in_dim | solution.py:523

commit v7 on v6

--- a/solution.py
+++ b/solution.py
@@ -26,8 +26,9 @@
 PAD = 4
 HEADS = 16
 ASK = HEADS * PAD
-WIDTH = (768, 1024)
+WIDTH = (768, 768, 256)
 TIGHT = HEADS * STEPS
+FAR = (2, 1, 3, 0)
 TOK = 16
 
 
@@ -56,7 +57,7 @@
     out,
     kt, wk, wv, wo, sl, slw, k_send, qv, lv, qf, lat,
     q_all, q_sib, q8_mine, q8, k8, o_sib, lt, o8_send, o8,
-    gath_a, gath_b, unpack, p_all, p_send, p_recv, p_sum, red,
+    gath_a, gath_b, gath_c, unpack, unpack_new, p_all, p_send, p_recv, p_sum, red,
     dma, sib_s, sib_r, sl_s, sl_r, z_s, z_r, ag_s, ag_r, red_s, red_r,
 ):
     g = lax.axis_index("grp")
@@ -64,7 +65,7 @@
     y, x = g // 4, g % 4
     z, c = h // 2, h % 2
     sib = (g, h + 1 - 2 * c)
-    gath = (gath_a, gath_b)
+    gath = (gath_a, gath_b, gath_c)
 
     load_sl = pltpu.make_async_copy(slices.at[:, pl.ds(TOK * z, TOK), :], sl, dma.at[1])
     load_qv = pltpu.make_async_copy(queries, qv, dma.at[8])
@@ -80,10 +81,19 @@
     load_kt[0].start()
 
     barrier = pltpu.get_barrier_semaphore()
-    for i in range(1, 16):
-        pl.semaphore_signal(barrier, inc=1, device_id=((g + i) % 16, h), device_id_type=MESH)
-    for i in range(1, 8):
-        pl.semaphore_signal(barrier, inc=1, device_id=(g, (h + i) % 8), device_id_type=MESH)
+    offsets = sorted(
+        ((dy, dx) for dy in range(4) for dx in range(4) if dy or dx),
+        key=lambda o: -min(o[0], 4 - o[0]) - min(o[1], 4 - o[1]),
+    )
+
+    def group_at(dy, dx):
+        return (y + dy) % 4 * 4 + (x + dx) % 4
+
+    for dy, dx in offsets:
+        pl.semaphore_signal(barrier, inc=1, device_id=(group_at(dy, dx), h), device_id_type=MESH)
+    for i in (2, 1, 3):
+        pl.semaphore_signal(barrier, inc=1, device_id=(g, 2 * ((z + i) % 4) + c), device_id_type=MESH)
+    pl.semaphore_signal(barrier, inc=1, device_id=sib, device_id_type=MESH)
 
     qf[...] = jnp.zeros_like(qf)
     lat[...] = jnp.zeros_like(lat)
@@ -144,25 +154,26 @@
     tight = jnp.where((tight[0] // STEPS == tight[1] // PAD) & (tight[0] % STEPS == tight[1] % PAD), 1.0, 0.0)
     q8_mine[...] = nn(tight.astype(BF16), q_all[8]).astype(BF16)
 
-    pl.semaphore_wait(barrier, 22)
+    pl.semaphore_wait(barrier, 19)
 
     ask_sib = remote(q_all.at[pl.ds(4 * (1 - c), 4)], q_sib, sib_s.at[0], sib_r.at[0], sib)
     ask_sib.start()
+
+    slice_sends = []
+    for i, (dy, dx) in enumerate(offsets):
+        to = group_at(dy, dx)
+        cp = remote(k_send.at[to], k8.at[c, pl.ds(TOK * g, TOK)], sl_s.at[i], sl_r.at[i], (to, h))
+        cp.start()
+        slice_sends.append(cp)
+    k8[c, pl.ds(TOK * g, TOK), :] = k_send[g]
+
     ask_z = []
-    for i in range(1, 4):
+    for i in (2, 1, 3):
         to = (z + i) % 4
         cp = remote(q8_mine, q8.at[z], z_s.at[i], z_r.at[i], (g, 2 * to + c))
         cp.start()
         ask_z.append(cp)
     q8[z] = q8_mine[...]
-
-    slice_sends = []
-    for i in range(1, 16):
-        to = (g + i) % 16
-        cp = remote(k_send.at[to], k8.at[c, pl.ds(TOK * g, TOK)], sl_s.at[i], sl_r.at[i], (to, h))
-        cp.start()
-        slice_sends.append(cp)
-    k8[c, pl.ds(TOK * g, TOK), :] = k_send[g]
 
     ask_sib.wait()
 
@@ -195,33 +206,35 @@
         return cp
 
     def values(part):
-        lo, count = (0, 4) if part == 0 else (4, 5)
+        count = 1 if part == 2 else 4
         rows = 16 * count
         head_of_row = lax.broadcasted_iota(jnp.int32, (rows, 512), 0) % 16 // PAD
         head_of_lane = lax.broadcasted_iota(jnp.int32, (rows, 512), 1) // VD
         mine = head_of_row == head_of_lane
         heads_out = []
         for quad in range(4):
-            lhs = lt[lo : lo + count, 16 * quad : 16 * quad + 16, :].reshape(rows, KV)
+            lhs = lt[4 * part : 4 * part + count, 16 * quad : 16 * quad + 16, :].reshape(rows, KV)
             rhs = jnp.concatenate([wv[4 * quad + j] for j in range(4)], axis=1)
             heads_out.append(jnp.where(mine, nn(lhs, rhs), 0.0).astype(BF16))
-        to_row = lax.broadcasted_iota(jnp.int32, (16, rows), 0)
-        from_row = lax.broadcasted_iota(jnp.int32, (16, rows), 1)
-
-        def picks(at):
-            return (at // STEPS == from_row // 16) & (at % STEPS == from_row % PAD)
-
-        blocks = []
-        if part == 0:
+        if part == 2:
+            to_row = lax.broadcasted_iota(jnp.int32, (16, 64), 0)
+            from_row = lax.broadcasted_iota(jnp.int32, (16, 64), 1)
+            spread = (to_row // 4 == from_row // 16) & (to_row % 4 == from_row % PAD) & (to_row % 4 < STEPS)
+            spread = jnp.where(spread, 1.0, 0.0).astype(BF16)
+            block = nn(spread, jnp.concatenate(heads_out, axis=0)).astype(BF16)
+        else:
+            to_row = lax.broadcasted_iota(jnp.int32, (16, rows), 0)
+            from_row = lax.broadcasted_iota(jnp.int32, (16, rows), 1)
+
+            def picks(at):
+                return (at // STEPS == from_row // 16) & (at % STEPS == from_row % PAD)
+
+            blocks = []
             direct = jnp.where((to_row < 12) & picks(to_row), 1.0, 0.0).astype(BF16)
             for b in range(3):
                 under = jnp.where((to_row >= 12) & picks(4 * b + to_row - 12), 1.0, 0.0).astype(BF16)
                 blocks.append(nn(direct, heads_out[b]) + nn(under, heads_out[3]))
-        else:
-            direct = jnp.where((to_row < 15) & picks(to_row), 1.0, 0.0).astype(BF16)
-            for b in range(4):
-                blocks.append(nn(direct, heads_out[b]))
-        block = jnp.concatenate(blocks, axis=1).astype(BF16)
+            block = jnp.concatenate(blocks, axis=1).astype(BF16)
         half = WIDTH[part]
         gath[part][0, 4 * y + x] = block[:, 0:half]
         gath[part][1, 4 * x + y] = block[:, half:]
@@ -255,40 +268,14 @@
                 ref = blocks_of(part, k, ring, d)
                 remote(ref, ref, ag_s.at[n], ag_r.at[n], along(ring if k == 0 else 1 - ring, d)).wait_recv()
 
-    def one_block(part, k, d1, d2):
-        one, two = (x, y) if k == 0 else (y, x)
-        return gath[part].at[k, pl.ds(4 * ((two - d2) % 4) + (one - d1) % 4, 1)]
-
-    def pass_on(part, k, d1):
-        ref = one_block(part, k, d1, 0)
-        for d in (2, 1, 3):
-            n = 32 + (k * 4 + d1) * 4 + d
-            cp = remote(ref, ref, ag_s.at[n], ag_r.at[n], along(1 - k, d))
-            cp.start()
-            ag_sends.append(cp)
-
-    def gather_blocks(part):
-        for d in (1, 3, 2):
-            for k in (0, 1):
-                n = ((part * 2 + k) * 2) * 4 + d
-                ref = blocks_of(part, k, 0, d)
-                remote(ref, ref, ag_s.at[n], ag_r.at[n], along(k, d)).wait_recv()
-                pass_on(part, k, d)
-
-    def gather_last(part):
-        for k in (0, 1):
-            for d1 in (0, 1, 3, 2):
-                for d2 in (1, 3, 2):
-                    n = 32 + (k * 4 + d1) * 4 + d2
-                    ref = one_block(part, k, d1, d2)
-                    remote(ref, ref, ag_s.at[n], ag_r.at[n], along(1 - k, d2)).wait_recv()
-
     def project(part):
         half = WIDTH[part]
         first_half = gath[part][0].reshape(256, half)
         second_half = jnp.concatenate([gath[part][1, 4 * (i % 4) + i // 4] for i in range(16)], axis=0)
         lhs = jnp.concatenate([first_half, second_half], axis=1)
-        if part == 0:
+        if part == 2:
+            lhs = jnp.concatenate([nn(unpack_new[b], lhs).astype(BF16) for b in range(4)], axis=1)
+        else:
             tall = jnp.concatenate([lhs[:, 512 * b : 512 * b + 512] for b in range(3)], axis=0)
             lhs = jnp.concatenate([lhs, nn(unpack[...], tall).astype(BF16)], axis=1)
         p_all[part] = nt(lhs, wo[...]).reshape(16, 16, 512)
@@ -306,13 +293,13 @@
 
     def hand(part, i):
         return remote(
-            p_sum.at[part, i], red.at[part, slot], red_s.at[8 * part + i], red_r.at[8 * part + slot],
-            (8 * c + i, keeper),
+            p_sum.at[part, i // 4 * 4 + (x + FAR[i % 4]) % 4], red.at[part, slot], red_s.at[8 * part + i], red_r.at[8 * part + slot],
+            (8 * c + i // 4 * 4 + (x + FAR[i % 4]) % 4, keeper),
         )
 
     def hand_out(part):
         for i in range(8):
-            to = 8 * c + i
+            to = 8 * c + i // 4 * 4 + (x + FAR[i % 4]) % 4
 
             @pl.when(jnp.logical_or(to != g, keeper != h))
             def _():
@@ -320,7 +307,7 @@
 
             @pl.when(jnp.logical_and(to == g, keeper == h))
             def _():
-                red[part, slot] = p_sum[part, i]
+                red[part, slot] = p_sum[part, i // 4 * 4 + (x + FAR[i % 4]) % 4]
 
     def take_in(part):
         half_of = g // 8
@@ -346,17 +333,20 @@
         mixed = jnp.concatenate([sums[0][:, 0:384], middle, shifted[:, 128:512]], axis=1)
         return mixed.astype(BF16)
 
-    lat_sends = [resident(0), resident(1)]
+    lat_sends = [resident(0), resident(1), resident(2)]
+    lat_sends[0].wait()
+    lat_sends[1].wait()
+    load_wv.wait()
+    values(0)
+    gather_send(0, 0)
 
     for cp in slice_sends:
         cp.wait()
     keys_sib = remote(k8.at[c], k8.at[c], sib_s.at[5], sib_r.at[5], sib)
     keys_sib.start()
-    for cp in lat_sends:
-        cp.wait()
-    load_wv.wait()
-    values(0)
-    gather_send(0, 0)
+    lat_sends.append(resident(3))
+    gather_wait(0, 0)
+    gather_send(0, 1)
 
     for cp in ask_z:
         cp.wait()
@@ -379,17 +369,17 @@
             stats = jnp.where(lane == 3 * n + t, piece, stats)
     o8_send[...] = jnp.concatenate([o, stats], axis=1).astype(BF16).reshape(4, TIGHT, WIDE)
     part_z = []
-    for i in range(1, 4):
+    for i in (2, 1, 3):
         to = (z + i) % 4
         cp = remote(o8_send.at[to], o8.at[z], z_s.at[3 + i], z_r.at[3 + i], (g, 2 * to + c))
         cp.start()
         part_z.append(cp)
     o8[z] = o8_send[z]
 
-    lat_sends = [resident(2)]
-    gather_wait(0, 0)
-    gather_send(0, 1)
-    lat_sends.append(resident(3))
+    lat_sends[2].wait()
+    lat_sends[3].wait()
+    values(1)
+    gather_send(1, 0)
 
     q = q8_mine[:, 0 : KV + ROPE]
     recent = lat[8].astype(BF16)
@@ -398,6 +388,8 @@
     e_new = jnp.exp((s_new - m_new) * SCALE)
     total_new = jnp.sum(e_new, axis=1, keepdims=True)
     o_new = nn(e_new.astype(BF16), recent[:, 0:KV])
+    gather_wait(1, 0)
+    gather_send(1, 1)
     for cp in part_z:
         cp.wait()
     m_part, total_part = [], []
@@ -418,38 +410,42 @@
     loose = (lax.broadcasted_iota(jnp.int32, (ASK, TIGHT), 0), lax.broadcasted_iota(jnp.int32, (ASK, TIGHT), 1))
     loose = jnp.where((loose[0] // PAD == loose[1] // STEPS) & (loose[0] % PAD == loose[1] % STEPS), 1.0, 0.0)
     lt[8] = nn(loose.astype(BF16), (o / total).astype(BF16)).astype(BF16)
-    for cp in lat_sends:
-        cp.wait()
-    values(1)
-    gather_send(1, 0)
-    for k in (0, 1):
-        pass_on(1, k, 0)
-    gather_blocks(1)
+    values(2)
+    gather_send(2, 0)
+
+    to_row = lax.broadcasted_iota(jnp.int32, (256, 256), 0)
+    from_row = lax.broadcasted_iota(jnp.int32, (256, 256), 1)
+    for b in range(4):
+        back = (to_row // 16 == from_row // 16) & (from_row % 16 == to_row % 16 + 4 * b) & (to_row % 16 < 4)
+        unpack_new[b] = jnp.where(back, 1.0, 0.0).astype(BF16)
 
     load_wo.wait()
     gather_wait(0, 1)
     swap = project(0)
+    gather_wait(2, 0)
+    gather_send(2, 1)
     add_cores(0, swap)
     hand_out(0)
-    gather_last(1)
-    swap = project(1)
-    sums_a = take_in(0)
-    add_cores(1, swap)
+    gather_wait(1, 1)
+    add_cores(1, project(1))
     hand_out(1)
-    sums_b = take_in(1)
-
-    to_row = lax.broadcasted_iota(jnp.int32, (16 * STEPS, 32), 0)
-    from_row = lax.broadcasted_iota(jnp.int32, (16 * STEPS, 32), 1)
+    gather_wait(2, 1)
+    add_cores(2, project(2))
+    hand_out(2)
+    sums = [take_in(0), take_in(1), take_in(2)]
+
+    to_row = lax.broadcasted_iota(jnp.int32, (16 * STEPS, 48), 0)
+    from_row = lax.broadcasted_iota(jnp.int32, (16 * STEPS, 48), 1)
     r = to_row % 16
-    source = jnp.where(r >= ROWS, 16 + 4 * STEPS, r // 2 % 2 * 16 + (r // 4 * 2 + r % 2) * STEPS) + to_row // 16
+    source = jnp.where(r >= ROWS, 32, r // 2 % 2 * 16 + (r // 4 * 2 + r % 2) * STEPS) + to_row // 16
     order = jnp.where(source == from_row, 1.0, 0.0).astype(BF16)
-    mixed = nn(order, jnp.concatenate([sums_a, sums_b], axis=0)).astype(BF16)
+    mixed = nn(order, jnp.concatenate(sums, axis=0)).astype(BF16)
     for t in range(STEPS):
         out[t] = mixed[16 * t : 16 * t + ROWS + 1]
 
-    for part in (0, 1):
+    for part in (0, 1, 2):
         for i in range(8):
-            pl.when(jnp.logical_or(8 * c + i != g, keeper != h))(hand(part, i).wait_send)
+            pl.when(jnp.logical_or(8 * c + i // 4 * 4 + (x + FAR[i % 4]) % 4 != g, keeper != h))(hand(part, i).wait_send)
     for cp in ag_sends:
         cp.wait_send()
 
@@ -487,23 +483,25 @@
             pltpu.VMEM((4, TIGHT, WIDE), BF16),
             pltpu.VMEM((2, 16, 16, WIDTH[0]), BF16),
             pltpu.VMEM((2, 16, 16, WIDTH[1]), BF16),
+            pltpu.VMEM((2, 16, 16, WIDTH[2]), BF16),
             pltpu.VMEM((256, 768), BF16),
-            pltpu.VMEM((2, 16, 16, 512), F32),
-            pltpu.VMEM((2, 8, 16, 512), BF16),
-            pltpu.VMEM((2, 8, 16, 512), BF16),
-            pltpu.VMEM((2, 8, 16, 512), BF16),
-            pltpu.VMEM((2, 8, 16, 512), BF16),
+            pltpu.VMEM((4, 256, 256), BF16),
+            pltpu.VMEM((3, 16, 16, 512), F32),
+            pltpu.VMEM((3, 8, 16, 512), BF16),
+            pltpu.VMEM((3, 8, 16, 512), BF16),
+            pltpu.VMEM((3, 8, 16, 512), BF16),
+            pltpu.VMEM((3, 8, 16, 512), BF16),
             sems((10,)),
-            sems((8,)),
-            sems((8,)),
+            sems((9,)),
+            sems((9,)),
             sems((16,)),
             sems((16,)),
             sems((7,)),
             sems((7,)),
-            sems((64,)),
-            sems((64,)),
-            sems((16,)),
-            sems((16,)),
+            sems((48,)),
+            sems((48,)),
+            sems((24,)),
+            sems((24,)),
         ],
         compiler_params=pltpu.CompilerParams(
             collective_id=0, has_side_effects=True, vmem_limit_bytes=56 * 1024 * 1024

time: 47.8 us -> 51.4 us (1.075)
  Pallas kernels: 46.1 us -> 49.7 us
    pallas_call x1, Pallas kernels: 46.1 us -> 49.7 us  [body(): pl.pallas_call(kernel, out_shape=jax.ShapeDtypeStruct((STEPS, ROWS + 1, 8...]
where the time goes in v7:
time: 51.4 us; the launch traced here: 51.2 us
  Pallas kernels  49.7 us (97%)
  local copies, waits for them, and re-layouts  1.54 us (3%)
    pallas_call x1, Pallas kernels, body(): pl.pallas_call(kernel, out_shape=jax.ShapeDtypeStruct((STEPS, ROWS + 1, 8...  49.7 us
    broadcast_in_dim x1, local copies, waits for them, and re-layouts, body(): return out[:, None]  1.54 us

profile of v7, /device:TPU:1, one launch (start us, length us, event | category | flops | bytes accessed | tf_op | source)
XLA Modules:
  0.0 51.2 jit_solution(11213189173076411858)
XLA Ops:
  0.0 49.7 %decode.1 = bf16[3,9,896]{2,1,0:T(8,128)(2,1)} custom-call(s32[1,8]{1,0:T(1,128)} %lengths.1, s32[1,16]{1,0:T(1,128)} %bitcast.17, bf16[9,3,3072]{2,1,0:T(4,128)(2,1)} %bitcast.15, bf16[9,3,576]{2,1,0:T(4,128)(2,1)} %bitcast.16, bf16[8,576,1536]{2,1,0:T(8,128)(2,1)} %bitcast.12, bf16[16,64,576]{2,1,0:T(8,128)(2,1)} %slices.1, bf16[16,128,512]{2,1,0:T(8,128)(2,1)} %w_key.1, ...), custom_call_target="tpu_custom_call" | custom-call | tf_op jit(solution)/shard_map/decode/pallas_call | solution.py:458
  49.7 1.5 %copy.10 = bf16[3,1,9,896]{3,0,2,1:T(4,128)(2,1)} copy(bf16[3,1,9,896]{3,2,0,1:T(8,128)(2,1)} %bitcast.14) | data formatting | bytes 96768 | tf_op jit(solution)/shard_map/broadcast_in_dim | solution.py:521

commit v8 on v6

--- a/solution.py
+++ b/solution.py
@@ -28,6 +28,7 @@
 ASK = HEADS * PAD
 WIDTH = (768, 1024)
 TIGHT = HEADS * STEPS
+FAR = (2, 1, 3, 0)
 TOK = 16
 
 
@@ -80,10 +81,19 @@
     load_kt[0].start()
 
     barrier = pltpu.get_barrier_semaphore()
-    for i in range(1, 16):
-        pl.semaphore_signal(barrier, inc=1, device_id=((g + i) % 16, h), device_id_type=MESH)
-    for i in range(1, 8):
-        pl.semaphore_signal(barrier, inc=1, device_id=(g, (h + i) % 8), device_id_type=MESH)
+    offsets = sorted(
+        ((dy, dx) for dy in range(4) for dx in range(4) if dy or dx),
+        key=lambda o: -min(o[0], 4 - o[0]) - min(o[1], 4 - o[1]),
+    )
+
+    def group_at(dy, dx):
+        return (y + dy) % 4 * 4 + (x + dx) % 4
+
+    for dy, dx in offsets:
+        pl.semaphore_signal(barrier, inc=1, device_id=(group_at(dy, dx), h), device_id_type=MESH)
+    for i in (2, 1, 3):
+        pl.semaphore_signal(barrier, inc=1, device_id=(g, 2 * ((z + i) % 4) + c), device_id_type=MESH)
+    pl.semaphore_signal(barrier, inc=1, device_id=sib, device_id_type=MESH)
 
     qf[...] = jnp.zeros_like(qf)
     lat[...] = jnp.zeros_like(lat)
@@ -144,25 +154,26 @@
     tight = jnp.where((tight[0] // STEPS == tight[1] // PAD) & (tight[0] % STEPS == tight[1] % PAD), 1.0, 0.0)
     q8_mine[...] = nn(tight.astype(BF16), q_all[8]).astype(BF16)
 
-    pl.semaphore_wait(barrier, 22)
+    pl.semaphore_wait(barrier, 19)
 
     ask_sib = remote(q_all.at[pl.ds(4 * (1 - c), 4)], q_sib, sib_s.at[0], sib_r.at[0], sib)
     ask_sib.start()
+
+    slice_sends = []
+    for i, (dy, dx) in enumerate(offsets):
+        to = group_at(dy, dx)
+        cp = remote(k_send.at[to], k8.at[c, pl.ds(TOK * g, TOK)], sl_s.at[i], sl_r.at[i], (to, h))
+        cp.start()
+        slice_sends.append(cp)
+    k8[c, pl.ds(TOK * g, TOK), :] = k_send[g]
+
     ask_z = []
-    for i in range(1, 4):
+    for i in (2, 1, 3):
         to = (z + i) % 4
         cp = remote(q8_mine, q8.at[z], z_s.at[i], z_r.at[i], (g, 2 * to + c))
         cp.start()
         ask_z.append(cp)
     q8[z] = q8_mine[...]
-
-    slice_sends = []
-    for i in range(1, 16):
-        to = (g + i) % 16
-        cp = remote(k_send.at[to], k8.at[c, pl.ds(TOK * g, TOK)], sl_s.at[i], sl_r.at[i], (to, h))
-        cp.start()
-        slice_sends.append(cp)
-    k8[c, pl.ds(TOK * g, TOK), :] = k_send[g]
 
     ask_sib.wait()
 
@@ -306,13 +317,13 @@
 
     def hand(part, i):
         return remote(
-            p_sum.at[part, i], red.at[part, slot], red_s.at[8 * part + i], red_r.at[8 * part + slot],
-            (8 * c + i, keeper),
+            p_sum.at[part, i // 4 * 4 + (x + FAR[i % 4]) % 4], red.at[part, slot], red_s.at[8 * part + i], red_r.at[8 * part + slot],
+            (8 * c + i // 4 * 4 + (x + FAR[i % 4]) % 4, keeper),
         )
 
     def hand_out(part):
         for i in range(8):
-            to = 8 * c + i
+            to = 8 * c + i // 4 * 4 + (x + FAR[i % 4]) % 4
 
             @pl.when(jnp.logical_or(to != g, keeper != h))
             def _():
@@ -320,7 +331,7 @@
 
             @pl.when(jnp.logical_and(to == g, keeper == h))
             def _():
-                red[part, slot] = p_sum[part, i]
+                red[part, slot] = p_sum[part, i // 4 * 4 + (x + FAR[i % 4]) % 4]
 
     def take_in(part):
         half_of = g // 8
@@ -379,7 +390,7 @@
             stats = jnp.where(lane == 3 * n + t, piece, stats)
     o8_send[...] = jnp.concatenate([o, stats], axis=1).astype(BF16).reshape(4, TIGHT, WIDE)
     part_z = []
-    for i in range(1, 4):
+    for i in (2, 1, 3):
         to = (z + i) % 4
         cp = remote(o8_send.at[to], o8.at[z], z_s.at[3 + i], z_r.at[3 + i], (g, 2 * to + c))
         cp.start()
@@ -433,9 +444,9 @@
     hand_out(0)
     gather_last(1)
     swap = project(1)
-    sums_a = take_in(0)
     add_cores(1, swap)
     hand_out(1)
+    sums_a = take_in(0)
     sums_b = take_in(1)
 
     to_row = lax.broadcasted_iota(jnp.int32, (16 * STEPS, 32), 0)
@@ -449,7 +460,7 @@
 
     for part in (0, 1):
         for i in range(8):
-            pl.when(jnp.logical_or(8 * c + i != g, keeper != h))(hand(part, i).wait_send)
+            pl.when(jnp.logical_or(8 * c + i // 4 * 4 + (x + FAR[i % 4]) % 4 != g, keeper != h))(hand(part, i).wait_send)
     for cp in ag_sends:
         cp.wait_send()
 

time: 47.8 us -> 46.9 us (0.981)
  Pallas kernels: 46.1 us -> 45.2 us
    pallas_call x1, Pallas kernels: 46.1 us -> 45.2 us  [body(): pl.pallas_call(kernel, out_shape=jax.ShapeDtypeStruct((STEPS, ROWS + 1, 8...]
where the time goes in v8:
time: 46.9 us; the launch traced here: 46.8 us
  Pallas kernels  45.2 us (96%)
  local copies, waits for them, and re-layouts  1.54 us (3%)
    pallas_call x1, Pallas kernels, body(): pl.pallas_call(kernel, out_shape=jax.ShapeDtypeStruct((STEPS, ROWS + 1, 8...  45.2 us
    broadcast_in_dim x1, local copies, waits for them, and re-layouts, body(): return out[:, None]  1.54 us

profile of v8, /device:TPU:1, one launch (start us, length us, event | category | flops | bytes accessed | tf_op | source)
XLA Modules:
  0.0 46.8 jit_solution(16223457543322217435)
XLA Ops:
  0.0 45.2 %decode.1 = bf16[3,9,896]{2,1,0:T(8,128)(2,1)} custom-call(s32[1,8]{1,0:T(1,128)} %lengths.1, s32[1,16]{1,0:T(1,128)} %bitcast.17, bf16[9,3,3072]{2,1,0:T(4,128)(2,1)} %bitcast.15, bf16[9,3,576]{2,1,0:T(4,128)(2,1)} %bitcast.16, bf16[8,576,1536]{2,1,0:T(8,128)(2,1)} %bitcast.12, bf16[16,64,576]{2,1,0:T(8,128)(2,1)} %slices.1, bf16[16,128,512]{2,1,0:T(8,128)(2,1)} %w_key.1, ...), custom_call_target="tpu_custom_call" | custom-call | tf_op jit(solution)/shard_map/decode/pallas_call | solution.py:473
  45.2 1.5 %copy.10 = bf16[3,1,9,896]{3,0,2,1:T(4,128)(2,1)} copy(bf16[3,1,9,896]{3,2,0,1:T(8,128)(2,1)} %bitcast.14) | data formatting | bytes 96768 | tf_op jit(solution)/shard_map/broadcast_in_dim | solution.py:534

commit v9 on v8

--- a/solution.py
+++ b/solution.py
@@ -75,10 +75,7 @@
     load_wv = pltpu.make_async_copy(w_value, wv, dma.at[6])
     load_wo = pltpu.make_async_copy(w_out, wo.at[0:448], dma.at[7])
     load_qv.start()
-    load_lv.start()
     load_wk.start()
-    load_sl.start()
-    load_kt[0].start()
 
     barrier = pltpu.get_barrier_semaphore()
     offsets = sorted(
@@ -94,6 +91,9 @@
     for i in (2, 1, 3):
         pl.semaphore_signal(barrier, inc=1, device_id=(g, 2 * ((z + i) % 4) + c), device_id_type=MESH)
     pl.semaphore_signal(barrier, inc=1, device_id=sib, device_id_type=MESH)
+    load_lv.start()
+    load_sl.start()
+    load_kt[0].start()
 
     qf[...] = jnp.zeros_like(qf)
     lat[...] = jnp.zeros_like(lat)

time: 46.9 us -> 46.9 us (level)
  no operation moved by 1% of the time
where the time goes in v9:
time: 46.9 us; the launch traced here: 46.8 us
  Pallas kernels  45.2 us (96%)
  local copies, waits for them, and re-layouts  1.54 us (3%)
    pallas_call x1, Pallas kernels, body(): pl.pallas_call(kernel, out_shape=jax.ShapeDtypeStruct((STEPS, ROWS + 1, 8...  45.2 us
    broadcast_in_dim x1, local copies, waits for them, and re-layouts, body(): return out[:, None]  1.54 us

profile of v9, /device:TPU:1, one launch (start us, length us, event | category | flops | bytes accessed | tf_op | source)
XLA Modules:
  0.0 46.8 jit_solution(16126858174654930083)
XLA Ops:
  0.0 45.2 %decode.1 = bf16[3,9,896]{2,1,0:T(8,128)(2,1)} custom-call(s32[1,8]{1,0:T(1,128)} %lengths.1, s32[1,16]{1,0:T(1,128)} %bitcast.17, bf16[9,3,3072]{2,1,0:T(4,128)(2,1)} %bitcast.15, bf16[9,3,576]{2,1,0:T(4,128)(2,1)} %bitcast.16, bf16[8,576,1536]{2,1,0:T(8,128)(2,1)} %bitcast.12, bf16[16,64,576]{2,1,0:T(8,128)(2,1)} %slices.1, bf16[16,128,512]{2,1,0:T(8,128)(2,1)} %w_key.1, ...), custom_call_target="tpu_custom_call" | custom-call | tf_op jit(solution)/shard_map/decode/pallas_call | solution.py:473
  45.2 1.5 %copy.10 = bf16[3,1,9,896]{3,0,2,1:T(4,128)(2,1)} copy(bf16[3,1,9,896]{3,2,0,1:T(8,128)(2,1)} %bitcast.14) | data formatting | bytes 96768 | tf_op jit(solution)/shard_map/broadcast_in_dim | solution.py:534
